TPU v7x, 128 devices: a whole 4x4x4 slice. The times are simulated.
128 devices in a mesh: frame: 2 (over core), video: 32 (over z, y, x_hi), score: 2 (over x_lo).
Axes of the slice: x: 4 (x_hi: 2, x_lo: 2; x = x_hi * 2 + x_lo), y: 4, z: 4, core: 2. Of those that a mesh axis runs over, the one named last changes fastest.
Arguments:
- queries: bfloat16 [2, 32, 512, 5120], P('frame', 'video', None, 'score'), may hold values from -120 to 120
- key_states: bfloat16 [2, 32, 512, 5120], P('frame', 'video', None, 'score'), may hold values from -4 to 4, as said below
- value_states: bfloat16 [2, 32, 512, 5120], P('frame', 'video', None, 'score'), may hold values from -32 to 32
- out_proj: bfloat16 [5120, 5120], P('score'), may hold values from -0.078125 to 0.078125
- noise_field: bfloat16 [2, 32, 512, 5120], P('frame', 'video', 'score'), may hold values from -6 to 6
- timesteps: int32 [2, 32], P('frame', 'video'), may hold values from 20 to 699
- routes: int32 [2, 32, 512, 1], P('frame', 'video', 'score'), may hold values from 0 to 63; in each aligned block of 256 rows (0 to 255, 256 to 511, ..., all dimensions but the last counted through in order) at most 8 rows name the same one
- modulation: float32 [64, 2, 5120], P(('video', 'score')), may hold values from -3 to 3
- context: float32 [32, 2, 5120], replicated, may hold values from -6 to 6
- guidance: float32 [32], replicated, may hold values from 1.5 to 6
- head_proj: bfloat16 [64, 5120, 64], P(('video', 'score')), may hold values from -0.078125 to 0.078125
Outputs:
- student_rows: bfloat16 [2, 32, 512, 5120], P('frame', 'video', 'score')
- guided_score: bfloat16 [2, 32, 512, 64], P('frame', 'video', 'score')
Inputs may be any that keep to these rules, and one draw needn't show every extreme that they name: `key_states`: row 1 of some blocks may nearly repeat row 0 of the same block. `routes`: among the 256 rows of one device no scorer appears more than 8 times.
All inputs are finite; a program needn't handle non-finite values.
Results may differ from a plain program's by a relative error of at most 0.014.
Values may be sent and summed in bfloat16 or wider, within the bound.
No kernel may reach another device: no remote copies, remote signals or barrier semaphores. Data moves between devices by JAX's collectives and lax.ppermute only.
A program may use at most 192 MiB of HBM per device.

v0:
```python
import functools
import math

import jax
import jax.numpy as jnp
from jax import lax
from jax.experimental import pallas as pl
from jax.experimental.pallas import tpu as pltpu
from jax.sharding import Mesh
from jax.sharding import PartitionSpec as P

HEAD_DIM = 128
CHUNKS = 4
HEAD_GROUP = 5
SCALE2 = HEAD_DIM ** (-0.5) * math.log2(math.e)
NT = (((1,), (1,)), ((), ()))
NN = (((1,), (0,)), ((), ()))
MIB = 1024 * 1024
CAP = 8
BF16 = jnp.bfloat16
F32 = jnp.float32


def dot_nt(a, b):
    return lax.dot_general(a, b, NT, preferred_element_type=F32)


def dot_nn(a, b):
    return lax.dot_general(a, b, NN, preferred_element_type=F32)


def params(mib=24):
    return pltpu.CompilerParams(vmem_limit_bytes=mib * MIB)


def cost(flops, moved):
    return pl.CostEstimate(flops=flops, bytes_accessed=moved, transcendentals=0)


def attend_kernel(info, q_ref, k_ref, v_ref, ke_ref, ve_ref, *refs):
    o_ref = refs[-1]
    later = info[1] == 1

    @pl.when(later)
    def both():
        for h in range(HEAD_GROUP):
            cols = slice(h * HEAD_DIM, (h + 1) * HEAD_DIM)
            q = q_ref[:, cols]
            s_own = dot_nt(q, k_ref[:, cols])
            s_early = dot_nt(q, ke_ref[:, cols])
            peak = jnp.maximum(
                jnp.max(s_own, axis=1, keepdims=True), jnp.max(s_early, axis=1, keepdims=True)
            )
            p_own = jnp.exp2((s_own - peak) * SCALE2)
            p_early = jnp.exp2((s_early - peak) * SCALE2)
            total = jnp.sum(p_own, axis=1, keepdims=True) + jnp.sum(p_early, axis=1, keepdims=True)
            acc = dot_nn(p_own.astype(BF16), v_ref[:, cols]) + dot_nn(
                p_early.astype(BF16), ve_ref[:, cols]
            )
            o_ref[:, cols] = (acc / total).astype(BF16)

    @pl.when(jnp.logical_not(later))
    def own():
        for h in range(HEAD_GROUP):
            cols = slice(h * HEAD_DIM, (h + 1) * HEAD_DIM)
            s_own = dot_nt(q_ref[:, cols], k_ref[:, cols])
            peak = jnp.max(s_own, axis=1, keepdims=True)
            p_own = jnp.exp2((s_own - peak) * SCALE2)
            total = jnp.sum(p_own, axis=1, keepdims=True)
            acc = dot_nn(p_own.astype(BF16), v_ref[:, cols])
            o_ref[:, cols] = (acc / total).astype(BF16)


def attend(half, frame, queries, keys, values, keys_early, values_early, earlier=()):
    tok, width = queries.shape
    rows = tok // 2
    wide = HEAD_GROUP * HEAD_DIM
    whole = pl.BlockSpec((tok, wide), lambda i, info: (0, i))
    early = pl.BlockSpec((tok, wide), lambda i, info: (0, i * info[1]))
    return pl.pallas_call(
        attend_kernel,
        grid_spec=pltpu.PrefetchScalarGridSpec(
            num_scalar_prefetch=1,
            grid=(width // wide,),
            in_specs=[pl.BlockSpec((rows, wide), lambda i, info: (info[0], i))]
            + [whole] * 2
            + [early] * 2
            + [pl.BlockSpec(memory_space=pl.ANY)] * len(earlier),
            out_specs=pl.BlockSpec((rows, wide), lambda i, info: (0, i)),
        ),
        out_shape=jax.ShapeDtypeStruct((rows, width), BF16),
        compiler_params=params(56),
        cost_estimate=cost(8 * rows * tok * width, 5 * tok * width * 2),
        name="attend",
    )(
        jnp.stack([half, frame]).astype(jnp.int32),
        queries,
        keys,
        values,
        keys_early,
        values_early,
        *earlier,
    )


def project_kernel(a_ref, w_ref, *refs):
    refs[-1][...] = dot_nn(a_ref[...], w_ref[...]).astype(BF16)


def project(a, w, start, count, earlier=(), tile=640):
    rows, depth = a.shape
    first = start // tile
    return pl.pallas_call(
        project_kernel,
        grid=(count // tile,),
        in_specs=[
            pl.BlockSpec((rows, depth), lambda i: (0, 0)),
            pl.BlockSpec((depth, tile), lambda i: (0, first + i)),
        ]
        + [pl.BlockSpec(memory_space=pl.ANY)] * len(earlier),
        out_specs=pl.BlockSpec((rows, tile), lambda i: (0, i)),
        out_shape=jax.ShapeDtypeStruct((rows, count), BF16),
        compiler_params=params(56),
        cost_estimate=cost(2 * rows * depth * count, depth * count * 2),
        name="project",
    )(a, w, *earlier)


def combine_kernel(groups, level, kept_ref, got_ref, noise_ref, picker_ref, *refs):
    rows_ref, picked = refs[-1 - groups], refs[-groups:]
    rows = (kept_ref[...].astype(F32) + got_ref[...].astype(F32)).astype(BF16)
    rows_ref[...] = rows
    s = level[0]
    noisy = ((1.0 - s) * rows.astype(F32) + s * noise_ref[...].astype(F32)).astype(BF16)
    slots = picked[0].shape[0]
    for d, ref in enumerate(picked):
        ref[...] = dot_nn(picker_ref[d * slots : (d + 1) * slots, :], noisy).astype(BF16)


def combine(level, kept, got, noise, picker, buffer, earlier, start, groups, tile=640):
    rows, count = got.shape
    first = start // tile
    places = picker.shape[0]
    slots = places // groups
    at = pl.BlockSpec((rows, tile), lambda i, s: (0, first + i))
    local = pl.BlockSpec((rows, tile), lambda i, s: (0, i))
    out = pl.BlockSpec((slots, tile), lambda i, s: (0, i))
    rest = ([] if buffer is None else [buffer]) + list(earlier)
    result = pl.pallas_call(
        functools.partial(combine_kernel, groups),
        grid_spec=pltpu.PrefetchScalarGridSpec(
            num_scalar_prefetch=1,
            grid=(count // tile,),
            in_specs=[
                at,
                local,
                at,
                pl.BlockSpec((places, rows), lambda i, s: (0, 0)),
            ]
            + [pl.BlockSpec(memory_space=pl.ANY)] * len(rest),
            out_specs=[at] + [out] * groups,
        ),
        out_shape=[jax.ShapeDtypeStruct(kept.shape, BF16)]
        + [jax.ShapeDtypeStruct((slots, count), BF16)] * groups,
        input_output_aliases={} if buffer is None else {5: 0},
        compiler_params=params(),
        cost_estimate=cost(2 * rows * places * count, rows * count * 10),
        name="combine",
    )(level, kept, got, noise, picker, *rest)
    return result[0], list(result[1:])


def teach_kernel(groups, feats, width, first, last, *refs):
    refs = list(refs)
    weight = refs[0]
    xs = refs[1 : 1 + groups]
    heads_ref, pieces_ref, ctx_ref = refs[1 + groups : 4 + groups]
    at = 4 + groups
    if not first:
        y_in, sq_in = refs[at : at + 2]
        at += 2
    if last:
        ids = refs[at : at + groups]
        shift_ref = refs[at + groups]
        at += groups + 1
        outs = refs[at : at + groups]
        y_ref, sq_ref = refs[at + groups :]
    else:
        y_ref, sq_ref = refs[at:]
    slots = xs[0].shape[0]
    tile = xs[0].shape[1]
    half = heads_ref.shape[0] // 2
    step = pl.program_id(0)

    @pl.when(step == 0)
    def start():
        if first:
            y_ref[...] = jnp.zeros_like(y_ref)
            sq_ref[...] = jnp.zeros_like(sq_ref)
        else:
            y_ref[...] = y_in[...]
            sq_ref[...] = sq_in[...]

    flat = jnp.concatenate([x[...] for x in xs] + [pieces_ref[...]], axis=0)
    y_ref[...] += dot_nt(flat, heads_ref[...])
    for d in range(groups):
        for c in range(2):
            total = sq_ref[c, d * slots : (d + 1) * slots, :]
            for j in range(tile // 128):
                cols = slice(j * 128, (j + 1) * 128)
                hidden = xs[d][:, cols].astype(F32) + ctx_ref[2 * d + c : 2 * d + c + 1, cols]
                total = total + hidden * hidden
            sq_ref[c, d * slots : (d + 1) * slots, :] = total

    if last:

        @pl.when(step == pl.num_programs(0) - 1)
        def finish():
            rows = groups * slots
            lane = lax.broadcasted_iota(jnp.int32, (8, 128), 1)
            ones = jnp.where(lane < 3, 1.0, 0.0).astype(BF16)
            shift = dot_nt(ones, shift_ref[...])[0:1]
            feat = lax.rem(lax.broadcasted_iota(jnp.int32, (half, 2 * feats), 0), feats)
            column = lax.broadcasted_iota(jnp.int32, (half, 2 * feats), 1)
            scorer = lax.broadcasted_iota(jnp.int32, (slots, half), 1) // feats
            for d in range(groups):
                at_rows = slice(d * slots, (d + 1) * slots)
                scale = [
                    lax.rsqrt(
                        jnp.sum(sq_ref[c, at_rows, :], axis=1, keepdims=True) / width + 1e-06
                    )
                    for c in range(2)
                ]
                w = weight[d]
                by_cond = w * scale[0]
                by_uncond = (1.0 - w) * scale[1]
                hit = ids[d][:, 0:1].astype(F32).astype(jnp.int32) == scorer
                result = jnp.zeros((slots, 2 * feats), F32)
                for part in range(2):
                    lanes = slice(part * half, (part + 1) * half)
                    bias = [
                        sum(
                            y_ref[
                                rows + p * 2 * groups + 2 * d + c : rows + p * 2 * groups + 2 * d + c + 1,
                                lanes,
                            ]
                            for p in range(3)
                        )
                        for c in range(2)
                    ]
                    full = (
                        (by_cond + by_uncond) * y_ref[at_rows, lanes]
                        + by_cond * bias[0]
                        + by_uncond * bias[1]
                        + shift[:, lanes]
                    )
                    full = jnp.where(hit, full, 0.0)
                    gather = jnp.where(feat + part * feats == column, 1.0, 0.0).astype(BF16)
                    high = full.astype(BF16)
                    low = (full - high.astype(F32)).astype(BF16)
                    result = result + dot_nn(high, gather) + dot_nn(low, gather)
                outs[d][...] = result.astype(BF16)


def teach(weight, xs, heads, pieces, ctx, carry, ids, start, feats, width, last, tile=640):
    groups = len(xs)
    slots, count = xs[0].shape
    half = heads.shape[0] // 2
    first = start // tile
    rows = groups * slots + pieces.shape[0]
    shapes = [
        jax.ShapeDtypeStruct((rows, 2 * half), F32),
        jax.ShapeDtypeStruct((2, groups * slots, 128), F32),
    ]
    fixed = [
        pl.BlockSpec((rows, 2 * half), lambda i, *s: (0, 0)),
        pl.BlockSpec((2, groups * slots, 128), lambda i, *s: (0, 0, 0)),
    ]

    def at(height):
        return pl.BlockSpec((height, tile), lambda i, *s: (0, first + i))

    in_specs = [pl.BlockSpec((slots, tile), lambda i, *s: (0, i))] * groups
    in_specs += [at(2 * half), at(pieces.shape[0]), at(ctx.shape[0])]
    operands = [weight, *xs, heads, pieces, ctx]
    if carry is not None:
        in_specs += fixed
        operands += list(carry)
    scratch = []
    if last:
        in_specs += [pl.BlockSpec((slots, 128), lambda i, *s: (0, 0))] * groups
        in_specs += [pl.BlockSpec((2 * half, 128), lambda i, *s: (0, width // 128))]
        operands += [*ids, heads]
        out_specs = [pl.BlockSpec((slots, 2 * feats), lambda i, *s: (0, 0))] * groups
        out_shape = [jax.ShapeDtypeStruct((slots, 2 * feats), BF16)] * groups
        scratch = [pltpu.VMEM(s.shape, s.dtype) for s in shapes]
    else:
        out_specs = fixed
        out_shape = shapes
    return pl.pallas_call(
        functools.partial(teach_kernel, groups, feats, width, carry is None, last),
        grid_spec=pltpu.PrefetchScalarGridSpec(
            num_scalar_prefetch=1,
            grid=(count // tile,),
            in_specs=in_specs,
            out_specs=out_specs,
            scratch_shapes=scratch,
        ),
        out_shape=out_shape,
        compiler_params=params(),
        cost_estimate=cost(4 * rows * half * count, 4 * half * count + 8 * rows * half),
        name="teach",
    )(*operands)


def unpick_kernel(picker_ref, *refs):
    slots = refs[0].shape[0]
    total = 0.0
    for d, ref in enumerate(refs[:-1]):
        total = total + dot_nn(picker_ref[:, d * slots : (d + 1) * slots], ref[...])
    refs[-1][...] = total.astype(BF16)


def unpick(picker_back, scores):
    rows = picker_back.shape[0]
    return pl.pallas_call(
        unpick_kernel,
        out_shape=jax.ShapeDtypeStruct((rows, scores[0].shape[1]), BF16),
        compiler_params=params(),
        name="unpick",
    )(picker_back, *scores)


def split3(x):
    high = lax.reduce_precision(x, 8, 7)
    rest = x - high
    mid = lax.reduce_precision(rest, 8, 7)
    low = rest - mid
    return high.astype(BF16), mid.astype(BF16), low.astype(BF16)


def shards(
    queries,
    key_states,
    value_states,
    out_proj,
    noise_field,
    timesteps,
    routes,
    modulation,
    context,
    guidance,
    head_proj,
):
    frame = lax.axis_index("frame")
    xl = lax.axis_index("xl")
    xh = lax.axis_index("xh")
    y_at = lax.axis_index("y")
    z_at = lax.axis_index("z")
    z_count = lax.axis_size("z")
    y_count = lax.axis_size("y")
    x_count = lax.axis_size("xh") * lax.axis_size("xl")
    q, k, v = queries[0, 0], key_states[0, 0], value_states[0, 0]
    width = out_proj.shape[1]
    half_rows = q.shape[0] // 2
    chunk = width // CHUNKS
    swap = [(0, 1), (1, 0)]

    def along(axis, count, d):
        return [(j, (j + d) % count) for j in range(count)]

    k_early = lax.ppermute(k, "frame", [(0, 1)])
    v_early = lax.ppermute(v, "frame", [(0, 1)])

    head = head_proj[0].astype(F32)
    feats = head.shape[1] // 2
    scaled = jnp.transpose(head * (1.0 + modulation[0, 0])[:, None]).astype(BF16)
    shift_out = jnp.sum(head * modulation[0, 1][:, None], axis=0)
    extra = jnp.pad(jnp.stack(split3(shift_out), axis=1), ((0, 0), (0, 125)))
    packed = jnp.concatenate([scaled, extra], axis=1)
    mine = lax.dynamic_slice_in_dim(packed, frame * feats, feats, 0)
    heads = lax.all_gather(mine, ("frame", "y", "xh", "xl"), axis=0, tiled=True)
    group = x_count * y_count

    targets = routes[0, 0, :, 0]
    towards = lax.rem(targets // group - z_at + z_count, z_count)
    scorer_y = lax.rem(targets // x_count, y_count)
    local = scorer_y * x_count + lax.rem(targets, x_count)
    slots = group * CAP
    same = towards[:, None] == towards[None, :]
    at = jnp.arange(half_rows, dtype=jnp.int32)
    rank = jnp.sum((same & (at[:, None] > at[None, :])).astype(jnp.int32), axis=1)
    place = towards * slots + rank
    places = jnp.arange(z_count * slots, dtype=jnp.int32)
    picker = (place[None, :] == places[:, None]).astype(BF16)
    picker_back = (place[:, None] == places[None, :]).astype(BF16)
    tags = jnp.where(place[None, :] == places[:, None], local.astype(F32)[None, :], 0.0)
    tags = jnp.pad(jnp.sum(tags, axis=1).astype(BF16)[:, None], ((0, 0), (0, 127)))
    tags = tags.reshape(z_count, slots, 128)
    ids = [tags[0]] + [
        lax.ppermute(tags[d], "z", along("z", z_count, d)) for d in range(1, z_count)
    ]

    z_from = [lax.rem(z_at - d + z_count, z_count) for d in range(z_count)]
    videos = jnp.stack([(z * y_count + y_at) * lax.axis_size("xh") + xh for z in z_from])
    ctx = context[videos].reshape(2 * z_count, width)
    weight = guidance[videos]
    pieces = jnp.pad(jnp.concatenate(split3(ctx), axis=0), ((0, 8), (0, 0)))
    level = timesteps[0].astype(F32) / 1000.0

    part_far = attend(1 - xl, frame, q, k, v, k_early, v_early)
    sent = []
    for c in range(CHUNKS):
        sent.append(project(part_far, out_proj, c * chunk, chunk, sent[-1:]))
    arrived = [lax.ppermute(one, "xl", swap) for one in sent]
    part_own = attend(xl, frame, q, k, v, k_early, v_early, sent[-1:])
    kept = project(part_own, out_proj, 0, width)

    student = None
    carry = None
    done = []
    for c in range(CHUNKS):
        student, blocks = combine(
            level,
            kept,
            arrived[c],
            noise_field[0, 0],
            picker,
            student,
            done[c - 2 : c - 1] if c > 1 else [],
            c * chunk,
            z_count,
        )
        got = [blocks[0]] + [
            lax.ppermute(blocks[d], "z", along("z", z_count, d)) for d in range(1, z_count)
        ]
        carry = teach(
            weight, got, heads, pieces, ctx, carry, ids, c * chunk, feats, width, c == CHUNKS - 1
        )
        done.append(carry[0])
    returned = [carry[0]] + [
        lax.ppermute(carry[d], "z", along("z", z_count, z_count - d)) for d in range(1, z_count)
    ]
    guided = unpick(picker_back, returned)
    return (student[None, None], guided[None, None])


def solution(mesh):
    z_count, y_count, x_high, x_low = 4, 4, 2, mesh.shape["score"]
    fine = Mesh(
        mesh.devices.reshape(mesh.shape["frame"], z_count, y_count, x_high, x_low),
        ("frame", "z", "y", "xh", "xl"),
    )
    video = ("z", "y", "xh")
    scorer = ("z", "y", "xh", "xl")
    in_specs = (
        P("frame", video, None, "xl"),
        P("frame", video, None, "xl"),
        P("frame", video, None, "xl"),
        P("xl", None),
        P("frame", video, "xl", None),
        P("frame", video),
        P("frame", video, "xl", None),
        P(scorer, None, None),
        P(),
        P(),
        P(scorer, None, None),
    )
    out_specs = (P("frame", video, "xl", None), P("frame", video, "xl", None))
    return jax.shard_map(shards, mesh=fine, in_specs=in_specs, out_specs=out_specs, check_vma=False)
```

profile of v0, /device:TPU:1, one launch (start us, length us, event | category | flops | bytes accessed | tf_op | source)
XLA Modules:
  0.0 181.4 jit_solution(1297538380591157422)
XLA Ops:
  15.7 2.2 %collective-permute-done.ke_ref = bf16[512,2560]{1,0:T(8,128)(2,1)} collective-permute-done((bf16[512,2560]{1,0:T(8,128)(2,1)}, bf16[512,2560]{1,0:T(8,128)(2,1)}, u32[]{:S(2)}, u32[]{:S(2)}) %collective-permute-start) | collective-permute-done | bytes 2621472 | tf_op jit(solution)/shard_map/ppermute | solution.py:372
  17.9 3.7 %collective-permute-done.1.ve_ref = bf16[512,2560]{1,0:T(8,128)(2,1)} collective-permute-done((bf16[512,2560]{1,0:T(8,128)(2,1)}, bf16[512,2560]{1,0:T(8,128)(2,1)}, u32[]{:S(2)}, u32[]{:S(2)}) %collective-permute-start.1) | collective-permute-done | bytes 2621472 | tf_op jit(solution)/shard_map/ppermute | solution.py:373
  21.7 13.7 %attend.2.a_ref = bf16[256,2560]{1,0:T(8,128)(2,1)} custom-call(s32[2]{0:T(128)} %get-tuple-element.87.info, bf16[512,2560]{1,0:T(8,128)(2,1)} %bitcast.40, bf16[512,2560]{1,0:T(8,128)(2,1)} %bitcast.43, bf16[512,2560]{1,0:T(8,128)(2,1)} %bitcast.46, bf16[512,2560]{1,0:T(8,128)(2,1)} %collective-permute-done.ke_ref, ...), custom_call_target="tpu_custom_call" | custom-call | flops 2684354560 | bytes 13107200 | tf_op jit(solution)/shard_map/attend/pallas_call | solution.py:80
  35.4 5.5 %project.5.refs_0_ = bf16[256,1280]{1,0:T(8,128)(2,1)} custom-call(bf16[256,2560]{1,0:T(8,128)(2,1)} %attend.2.a_ref, bf16[2560,5120]{1,0:T(8,128)(2,1)} %w_ref.9), custom_call_target="tpu_custom_call" | custom-call | flops 1677721600 | bytes 6553600 | tf_op jit(solution)/shard_map/project/pallas_call | solution.py:113
  40.9 1.8 collective-permute-start.5
  42.7 5.5 %project.6.refs_0_ = bf16[256,1280]{1,0:T(8,128)(2,1)} custom-call(bf16[256,2560]{1,0:T(8,128)(2,1)} %attend.2.a_ref, bf16[2560,5120]{1,0:T(8,128)(2,1)} %w_ref.9, bf16[256,1280]{1,0:T(8,128)(2,1)} %project.5.refs_0_), custom_call_target="tpu_custom_call" | custom-call | flops 1677721600 | bytes 6553600 | tf_op jit(solution)/shard_map/project/pallas_call | solution.py:113
  48.1 5.5 %project.7.refs_0_ = bf16[256,1280]{1,0:T(8,128)(2,1)} custom-call(bf16[256,2560]{1,0:T(8,128)(2,1)} %attend.2.a_ref, bf16[2560,5120]{1,0:T(8,128)(2,1)} %w_ref.9, bf16[256,1280]{1,0:T(8,128)(2,1)} %project.6.refs_0_), custom_call_target="tpu_custom_call" | custom-call | flops 1677721600 | bytes 6553600 | tf_op jit(solution)/shard_map/project/pallas_call | solution.py:113
  55.1 5.7 %project.8.refs_0_ = bf16[256,1280]{1,0:T(8,128)(2,1)} custom-call(bf16[256,2560]{1,0:T(8,128)(2,1)} %attend.2.a_ref, bf16[2560,5120]{1,0:T(8,128)(2,1)} %w_ref.9, bf16[256,1280]{1,0:T(8,128)(2,1)} %project.7.refs_0_), custom_call_target="tpu_custom_call" | custom-call | flops 1677721600 | bytes 6553600 | tf_op jit(solution)/shard_map/project/pallas_call | solution.py:113
  60.8 13.6 %attend.3.a_ref = bf16[256,2560]{1,0:T(8,128)(2,1)} custom-call(s32[2]{0:T(128)} %get-tuple-element.86.info, bf16[512,2560]{1,0:T(8,128)(2,1)} %bitcast.41, bf16[512,2560]{1,0:T(8,128)(2,1)} %bitcast.44, bf16[512,2560]{1,0:T(8,128)(2,1)} %bitcast.47, bf16[512,2560]{1,0:T(8,128)(2,1)} %collective-permute-done.ke_ref, ...), custom_call_target="tpu_custom_call" | custom-call | flops 2684354560 | bytes 13107200 | tf_op jit(solution)/shard_map/attend/pallas_call | solution.py:80
  74.4 15.9 %project.9.kept_ref = bf16[256,5120]{1,0:T(8,128)(2,1)} custom-call(bf16[256,2560]{1,0:T(8,128)(2,1)} %attend.3.a_ref, bf16[2560,5120]{1,0:T(8,128)(2,1)} %w_ref.9), custom_call_target="tpu_custom_call" | custom-call | flops 6710886400 | bytes 26214400 | tf_op jit(solution)/shard_map/project/pallas_call | solution.py:113
  92.0 2.1 %combine.4 = (bf16[256,5120]{1,0:T(8,128)(2,1)}, bf16[128,1280]{1,0:T(8,128)(2,1)S(1)}, bf16[128,1280]{1,0:T(8,128)(2,1)}, bf16[128,1280]{1,0:T(8,128)(2,1)}, bf16[128,1280]{1,0:T(8,128)(2,1)}) custom-call(f32[1]{0:T(128)} %bitcast.level, bf16[256,5120]{1,0:T(8,128)(2,1)S(1)} %copy-done.3, bf16[256,1280]{1,0:T(8,128)(2,1)S(1)} %collective-permute-done.5.got_ref, ...), custom_call_target="tpu_custom_call" | custom-call | flops 335544320 | bytes 3276800 | tf_op jit(solution)/shard_map/combine/pallas_call | solution.py:149
  94.9 2.3 %collective-permute-start.6 = (bf16[128,1280]{1,0:T(8,128)(2,1)}, bf16[128,1280]{1,0:T(8,128)(2,1)}, u32[]{:S(2)}, u32[]{:S(2)}) collective-permute-start(bf16[128,1280]{1,0:T(8,128)(2,1)} %get-tuple-element.35), channel_id=1, source_target_pairs={{0,16},{16,32},{32,48},{48,0},{1,17},{17,33},{33,49},{49,1},{2,18}... | collective-permute-start | bytes 983048 | tf_op jit(solution)/shard_map/ppermute | solution.py:435
  97.2 3.6 %collective-permute-start.7 = (bf16[128,1280]{1,0:T(8,128)(2,1)}, bf16[128,1280]{1,0:T(8,128)(2,1)}, u32[]{:S(2)}, u32[]{:S(2)}) collective-permute-start(bf16[128,1280]{1,0:T(8,128)(2,1)} %get-tuple-element.36), channel_id=1, source_target_pairs={{0,32},{16,48},{32,0},{48,16},{1,33},{17,49},{33,1},{49,17},{2,34}... | collective-permute-start | bytes 983048 | tf_op jit(solution)/shard_map/ppermute | solution.py:435
  102.7 1.7 copy-done.6
  105.5 2.1 %combine.5 = (bf16[256,5120]{1,0:T(8,128)(2,1)}, bf16[128,1280]{1,0:T(8,128)(2,1)S(1)}, bf16[128,1280]{1,0:T(8,128)(2,1)}, bf16[128,1280]{1,0:T(8,128)(2,1)}, bf16[128,1280]{1,0:T(8,128)(2,1)}) custom-call(f32[1]{0:T(128)} %bitcast.level, bf16[256,5120]{1,0:T(8,128)(2,1)S(1)} %copy-done.4, ...), custom_call_target="tpu_custom_call", output_to_operand_aliasing={{0}: (5, {})} | custom-call | flops 335544320 | bytes 3276800 | tf_op jit(solution)/shard_map/combine/pallas_call | solution.py:149
  109.4 5.4 %collective-permute-done.7.refs_3_ = bf16[128,1280]{1,0:T(8,128)(2,1)} collective-permute-done((bf16[128,1280]{1,0:T(8,128)(2,1)}, bf16[128,1280]{1,0:T(8,128)(2,1)}, u32[]{:S(2)}, u32[]{:S(2)}) %collective-permute-start.7) | collective-permute-done | bytes 327712 | tf_op jit(solution)/shard_map/ppermute | solution.py:435
  114.9 4.0 %copy-done.2 = bf16[1024,5248]{1,0:T(8,128)(2,1)S(1)} copy-done((bf16[1024,5248]{1,0:T(8,128)(2,1)S(1)}, bf16[1024,5248]{1,0:T(8,128)(2,1)}, u32[]{:S(2)}) %copy-start.2) | copy-done | bytes 10747928
  119.9 4.9 %teach.4 = (f32[544,1024]{1,0:T(8,128)S(1)}, f32[2,512,128]{2,1,0:T(8,128)S(1)}) custom-call(f32[4]{0:T(128)S(1)} %gather_fusion, bf16[128,1280]{1,0:T(8,128)(2,1)S(1)} %copy-done.11, bf16[128,1280]{1,0:T(8,128)(2,1)} %collective-permute-done.6.refs_2_, bf16[128,1280]{1,0:T(8,128)(2,1)} %collective-permute-done.7.refs_3_, ...), custom_call_target="tpu_custom_call" | custom-call | flops 1426063360 | bytes 4849664 | tf_op jit(solution)/shard_map/teach/pallas_call | solution.py:300
  124.9 2.7 %combine.6 = (bf16[256,5120]{1,0:T(8,128)(2,1)}, bf16[128,1280]{1,0:T(8,128)(2,1)S(1)}, bf16[128,1280]{1,0:T(8,128)(2,1)S(1)}, bf16[128,1280]{1,0:T(8,128)(2,1)S(1)}, bf16[128,1280]{1,0:T(8,128)(2,1)S(1)}) custom-call(f32[1]{0:T(128)} %bitcast.level, bf16[256,5120]{1,0:T(8,128)(2,1)S(1)} %copy-done.4, ...), custom_call_target="tpu_custom_call", output_to_operand_aliasing={{0}: (5, {})} | custom-call | flops 335544320 | bytes 3276800 | tf_op jit(solution)/shard_map/combine/pallas_call | solution.py:149
  130.7 1.9 %collective-permute-start.16 = (bf16[128,1280]{1,0:T(8,128)(2,1)S(1)}, bf16[128,1280]{1,0:T(8,128)(2,1)S(1)}, u32[]{:S(2)}, u32[]{:S(2)}) collective-permute-start(bf16[128,1280]{1,0:T(8,128)(2,1)S(1)} %get-tuple-element.53), channel_id=1, source_target_pairs={{0,32},{16,48},{32,0},{48,16},{1,33},{17,49},{33,1},{49,17},{2,34}... | collective-permute-start | bytes 983048 | tf_op jit(solution)/shard_map/ppermute | solution.py:435
  132.6 2.0 %collective-permute-start.17 = (bf16[128,1280]{1,0:T(8,128)(2,1)S(1)}, bf16[128,1280]{1,0:T(8,128)(2,1)S(1)}, u32[]{:S(2)}, u32[]{:S(2)}) collective-permute-start(bf16[128,1280]{1,0:T(8,128)(2,1)S(1)} %get-tuple-element.54), channel_id=1, source_target_pairs={{0,48},{16,0},{32,16},{48,32},{1,49},{17,1},{33,17},{49,33},{2,50}... | collective-permute-start | bytes 983048 | tf_op jit(solution)/shard_map/ppermute | solution.py:435
  134.6 4.7 %teach.5 = (f32[544,1024]{1,0:T(8,128)S(1)}, f32[2,512,128]{2,1,0:T(8,128)S(1)}) custom-call(f32[4]{0:T(128)S(1)} %gather_fusion, bf16[128,1280]{1,0:T(8,128)(2,1)S(1)} %copy-done.13, bf16[128,1280]{1,0:T(8,128)(2,1)} %collective-permute-done.9.refs_2_, bf16[128,1280]{1,0:T(8,128)(2,1)} %collective-permute-done.10.refs_3_, ...), custom_call_target="tpu_custom_call" | custom-call | flops 1426063360 | bytes 4849664 | tf_op jit(solution)/shard_map/teach/pallas_call | solution.py:300
  139.2 2.6 %combine.7 = (bf16[256,5120]{1,0:T(8,128)(2,1)}, bf16[128,1280]{1,0:T(8,128)(2,1)S(1)}, bf16[128,1280]{1,0:T(8,128)(2,1)S(1)}, bf16[128,1280]{1,0:T(8,128)(2,1)S(1)}, bf16[128,1280]{1,0:T(8,128)(2,1)S(1)}) custom-call(f32[1]{0:T(128)} %bitcast.level, bf16[256,5120]{1,0:T(8,128)(2,1)S(1)} %copy-done.4, ...), custom_call_target="tpu_custom_call", output_to_operand_aliasing={{0}: (5, {})} | custom-call | flops 335544320 | bytes 3276800 | tf_op jit(solution)/shard_map/combine/pallas_call | solution.py:149
  141.8 2.4 %collective-permute-start.13 = (bf16[128,1280]{1,0:T(8,128)(2,1)S(1)}, bf16[128,1280]{1,0:T(8,128)(2,1)S(1)}, u32[]{:S(2)}, u32[]{:S(2)}) collective-permute-start(bf16[128,1280]{1,0:T(8,128)(2,1)S(1)} %get-tuple-element.49), channel_id=1, source_target_pairs={{0,32},{16,48},{32,0},{48,16},{1,33},{17,49},{33,1},{49,17},{2,34}... | collective-permute-start | bytes 983048 | tf_op jit(solution)/shard_map/ppermute | solution.py:435
  144.7 2.2 %collective-permute-start.19 = (bf16[128,128]{1,0:T(8,128)(2,1)S(1)}, bf16[128,128]{1,0:T(8,128)(2,1)S(1)}, u32[]{:S(2)}, u32[]{:S(2)}) collective-permute-start(bf16[128,128]{1,0:T(8,128)(2,1)S(1)} %get-tuple-element.77), channel_id=1, source_target_pairs={{0,32},{16,48},{32,0},{48,16},{1,33},{17,49},{33,1},{49,17},{2,34}... | collective-permute-start | bytes 98312 | tf_op jit(solution)/shard_map/ppermute | solution.py:401
  146.9 2.7 %collective-permute-done.17.refs_4_ = bf16[128,1280]{1,0:T(8,128)(2,1)S(1)} collective-permute-done((bf16[128,1280]{1,0:T(8,128)(2,1)S(1)}, bf16[128,1280]{1,0:T(8,128)(2,1)S(1)}, u32[]{:S(2)}, u32[]{:S(2)}) %collective-permute-start.17) | collective-permute-done | bytes 327712 | tf_op jit(solution)/shard_map/ppermute | solution.py:435
  149.6 4.0 %collective-permute-start.20 = (bf16[128,128]{1,0:T(8,128)(2,1)S(1)}, bf16[128,128]{1,0:T(8,128)(2,1)S(1)}, u32[]{:S(2)}, u32[]{:S(2)}) collective-permute-start(bf16[128,128]{1,0:T(8,128)(2,1)S(1)} %get-tuple-element.75), channel_id=1, source_target_pairs={{0,48},{16,0},{32,16},{48,32},{1,49},{17,1},{33,17},{49,33},{2,50}... | collective-permute-start | bytes 98312 | tf_op jit(solution)/shard_map/ppermute | solution.py:401
  153.6 4.0 %teach.6 = (f32[544,1024]{1,0:T(8,128)S(1)}, f32[2,512,128]{2,1,0:T(8,128)S(1)}) custom-call(f32[4]{0:T(128)S(1)} %gather_fusion, bf16[128,1280]{1,0:T(8,128)(2,1)S(1)} %get-tuple-element.51.refs_1_, bf16[128,1280]{1,0:T(8,128)(2,1)S(1)} %collective-permute-done.15.refs_2_, bf16[128,1280]{1,0:T(8,128)(2,1)S(1)} %collective-permute-done.16.refs_3_, ...), custom_call_target="tpu_custom_call" | custom-call | flops 1426063360 | bytes 4849664 | tf_op jit(solution)/shard_map/teach/pallas_call | solution.py:300
  158.0 2.4 %collective-permute-done.20.refs_13_ = bf16[128,128]{1,0:T(8,128)(2,1)S(1)} collective-permute-done((bf16[128,128]{1,0:T(8,128)(2,1)S(1)}, bf16[128,128]{1,0:T(8,128)(2,1)S(1)}, u32[]{:S(2)}, u32[]{:S(2)}) %collective-permute-start.20) | collective-permute-done | bytes 32800 | tf_op jit(solution)/shard_map/ppermute | solution.py:401
  160.4 5.6 %teach.7 = (bf16[128,64]{1,0:T(8,128)(2,1)S(1)}, bf16[128,64]{1,0:T(8,128)(2,1)S(1)}, bf16[128,64]{1,0:T(8,128)(2,1)S(1)}, bf16[128,64]{1,0:T(8,128)(2,1)S(1)}) custom-call(f32[4]{0:T(128)S(1)} %gather_fusion, bf16[128,1280]{1,0:T(8,128)(2,1)S(1)} %get-tuple-element.47.refs_1_, bf16[128,1280]{1,0:T(8,128)(2,1)S(1)} %collective-permute-done.12.refs_2_, ...), custom_call_target="tpu_custom_call" | custom-call | flops 1426063360 | bytes 4849664 | tf_op jit(solution)/shard_map/teach/pallas_call | solution.py:300
  166.0 2.4 %collective-permute-start.21 = (bf16[128,64]{1,0:T(8,128)(2,1)S(1)}, bf16[128,64]{1,0:T(8,128)(2,1)S(1)}, u32[]{:S(2)}, u32[]{:S(2)}) collective-permute-start(bf16[128,64]{1,0:T(8,128)(2,1)S(1)} %get-tuple-element.59), channel_id=1, source_target_pairs={{0,48},{16,0},{32,16},{48,32},{1,49},{17,1},{33,17},{49,33},{2,50}... | collective-permute-start | bytes 49160 | tf_op jit(solution)/shard_map/ppermute | solution.py:442
  169.4 3.2 %collective-permute-done.22.refs_2_ = bf16[128,64]{1,0:T(8,128)(2,1)S(1)} collective-permute-done((bf16[128,64]{1,0:T(8,128)(2,1)S(1)}, bf16[128,64]{1,0:T(8,128)(2,1)S(1)}, u32[]{:S(2)}, u32[]{:S(2)}) %collective-permute-start.22) | collective-permute-done | bytes 16416 | tf_op jit(solution)/shard_map/ppermute | solution.py:442
  (97 shorter events, 24.3 us)
Async XLA Ops:
  7.2 107.7 %all-gather.2.cloned.1.call-start = ((), (), s32[]{:S(2)}) async-start(), calls=%async_computation | async-start | bytes 11083776 | tf_op jit(solution)/shard_map/all_gather | solution.py:382
  10.5 7.4 %collective-permute-start = (bf16[512,2560]{1,0:T(8,128)(2,1)}, bf16[512,2560]{1,0:T(8,128)(2,1)}, u32[]{:S(2)}, u32[]{:S(2)}) collective-permute-start(bf16[512,2560]{1,0:T(8,128)(2,1)} %bitcast.42), channel_id=1, source_target_pairs={{0,64},{1,65},{2,66},{3,67},{4,68},{5,69},{6,70},{7,71},{8,72},{9,... | collective-permute-start | bytes 7864328 | tf_op jit(solution)/shard_map/ppermute | solution.py:372
  11.8 9.9 %collective-permute-start.1 = (bf16[512,2560]{1,0:T(8,128)(2,1)}, bf16[512,2560]{1,0:T(8,128)(2,1)}, u32[]{:S(2)}, u32[]{:S(2)}) collective-permute-start(bf16[512,2560]{1,0:T(8,128)(2,1)} %bitcast.45), channel_id=1, source_target_pairs={{0,64},{1,65},{2,66},{3,67},{4,68},{5,69},{6,70},{7,71},{8,72},{9,... | collective-permute-start | bytes 7864328 | tf_op jit(solution)/shard_map/ppermute | solution.py:373
  40.9 49.4 %collective-permute-start.5 = (bf16[256,1280]{1,0:T(8,128)(2,1)}, bf16[256,1280]{1,0:T(8,128)(2,1)S(1)}, u32[]{:S(2)}, u32[]{:S(2)}) collective-permute-start(bf16[256,1280]{1,0:T(8,128)(2,1)} %project.5.refs_0_), channel_id=1, source_target_pairs={{0,1},{1,0},{2,3},{3,2},{4,5},{5,4},{6,7},{7,6},{8,9},{9,8},{10,11... | collective-permute-start | bytes 1966088 | tf_op jit(solution)/shard_map/ppermute | solution.py:415
  48.1 52.7 %collective-permute-start.4 = (bf16[256,1280]{1,0:T(8,128)(2,1)}, bf16[256,1280]{1,0:T(8,128)(2,1)S(1)}, u32[]{:S(2)}, u32[]{:S(2)}) collective-permute-start(bf16[256,1280]{1,0:T(8,128)(2,1)} %project.6.refs_0_), channel_id=1, source_target_pairs={{0,1},{1,0},{2,3},{3,2},{4,5},{5,4},{6,7},{7,6},{8,9},{9,8},{10,11... | collective-permute-start | bytes 1966088 | tf_op jit(solution)/shard_map/ppermute | solution.py:415
  53.6 71.3 %collective-permute-start.3 = (bf16[256,1280]{1,0:T(8,128)(2,1)}, bf16[256,1280]{1,0:T(8,128)(2,1)}, u32[]{:S(2)}, u32[]{:S(2)}) collective-permute-start(bf16[256,1280]{1,0:T(8,128)(2,1)} %project.7.refs_0_), channel_id=1, source_target_pairs={{0,1},{1,0},{2,3},{3,2},{4,5},{5,4},{6,7},{7,6},{8,9},{9,8},{10,11... | collective-permute-start | bytes 1966088 | tf_op jit(solution)/shard_map/ppermute | solution.py:415
  60.8 78.5 %collective-permute-start.2 = (bf16[256,1280]{1,0:T(8,128)(2,1)}, bf16[256,1280]{1,0:T(8,128)(2,1)}, u32[]{:S(2)}, u32[]{:S(2)}) collective-permute-start(bf16[256,1280]{1,0:T(8,128)(2,1)} %project.8.refs_0_), channel_id=1, source_target_pairs={{0,1},{1,0},{2,3},{3,2},{4,5},{5,4},{6,7},{7,6},{8,9},{9,8},{10,11... | collective-permute-start | bytes 1966088 | tf_op jit(solution)/shard_map/ppermute | solution.py:415
  74.4 15.9 %copy-start.5 = (bf16[1,1,256,5120]{3,2,1,0:T(8,128)(2,1)S(1)}, bf16[1,1,256,5120]{3,2,1,0:T(8,128)(2,1)}, u32[]{:S(2)}) copy-start(bf16[1,1,256,5120]{3,2,1,0:T(8,128)(2,1)} %param.15) | copy-start | bytes 7864324
  92.0 10.0 %copy-start.14 = (f32[32]{0:T(128)S(1)}, f32[32]{0:T(128)}, u32[]{:S(2)}) copy-start(f32[32]{0:T(128)} %param.20) | copy-start | bytes 388
  92.0 10.7 %copy-start.4 = (bf16[256,5120]{1,0:T(8,128)(2,1)S(1)}, bf16[256,5120]{1,0:T(8,128)(2,1)}, u32[]{:S(2)}) copy-start(bf16[256,5120]{1,0:T(8,128)(2,1)} %project.9.kept_ref) | copy-start | bytes 7864324
  94.9 13.5 %collective-permute-start.6 = (bf16[128,1280]{1,0:T(8,128)(2,1)}, bf16[128,1280]{1,0:T(8,128)(2,1)}, u32[]{:S(2)}, u32[]{:S(2)}) collective-permute-start(bf16[128,1280]{1,0:T(8,128)(2,1)} %get-tuple-element.35), channel_id=1, source_target_pairs={{0,16},{16,32},{32,48},{48,0},{1,17},{17,33},{33,49},{49,1},{2,18}... | collective-permute-start | bytes 983048 | tf_op jit(solution)/shard_map/ppermute | solution.py:435
  97.2 17.7 %collective-permute-start.7 = (bf16[128,1280]{1,0:T(8,128)(2,1)}, bf16[128,1280]{1,0:T(8,128)(2,1)}, u32[]{:S(2)}, u32[]{:S(2)}) collective-permute-start(bf16[128,1280]{1,0:T(8,128)(2,1)} %get-tuple-element.36), channel_id=1, source_target_pairs={{0,32},{16,48},{32,0},{48,16},{1,33},{17,49},{33,1},{49,17},{2,34}... | collective-permute-start | bytes 983048 | tf_op jit(solution)/shard_map/ppermute | solution.py:435
  101.6 13.2 %collective-permute-start.8 = (bf16[128,1280]{1,0:T(8,128)(2,1)}, bf16[128,1280]{1,0:T(8,128)(2,1)}, u32[]{:S(2)}, u32[]{:S(2)}) collective-permute-start(bf16[128,1280]{1,0:T(8,128)(2,1)} %get-tuple-element.37), channel_id=1, source_target_pairs={{0,48},{16,0},{32,16},{48,32},{1,49},{17,1},{33,17},{49,33},{2,50}... | collective-permute-start | bytes 983048 | tf_op jit(solution)/shard_map/ppermute | solution.py:435
  108.4 21.1 %collective-permute-start.9 = (bf16[128,1280]{1,0:T(8,128)(2,1)}, bf16[128,1280]{1,0:T(8,128)(2,1)}, u32[]{:S(2)}, u32[]{:S(2)}) collective-permute-start(bf16[128,1280]{1,0:T(8,128)(2,1)} %get-tuple-element.41), channel_id=1, source_target_pairs={{0,16},{16,32},{32,48},{48,0},{1,17},{17,33},{33,49},{49,1},{2,18}... | collective-permute-start | bytes 983048 | tf_op jit(solution)/shard_map/ppermute | solution.py:435
  114.9 15.8 %collective-permute-start.10 = (bf16[128,1280]{1,0:T(8,128)(2,1)}, bf16[128,1280]{1,0:T(8,128)(2,1)}, u32[]{:S(2)}, u32[]{:S(2)}) collective-permute-start(bf16[128,1280]{1,0:T(8,128)(2,1)} %get-tuple-element.42), channel_id=1, source_target_pairs={{0,32},{16,48},{32,0},{48,16},{1,33},{17,49},{33,1},{49,17},{2,34}... | collective-permute-start | bytes 983048 | tf_op jit(solution)/shard_map/ppermute | solution.py:435
  114.9 17.7 %collective-permute-start.11 = (bf16[128,1280]{1,0:T(8,128)(2,1)}, bf16[128,1280]{1,0:T(8,128)(2,1)}, u32[]{:S(2)}, u32[]{:S(2)}) collective-permute-start(bf16[128,1280]{1,0:T(8,128)(2,1)} %get-tuple-element.43), channel_id=1, source_target_pairs={{0,48},{16,0},{32,16},{48,32},{1,49},{17,1},{33,17},{49,33},{2,50}... | collective-permute-start | bytes 983048 | tf_op jit(solution)/shard_map/ppermute | solution.py:435
  119.9 14.6 %slice-start = ((s8[10747904]{0:T(1024)(128)(4,1)}), s8[4194304]{0:T(1024)(128)(4,1)S(1)}, s32[]{:S(2)}) async-start(s8[10747904]{0:T(1024)(128)(4,1)} %bitcast.32), calls=%async_computation.1 | async-start | bytes 8388608
  119.9 14.6 %slice-start.1 = ((s8[10747904]{0:T(1024)(128)(4,1)}), s8[4194304]{0:T(1024)(128)(4,1)S(1)}, s32[]{:S(2)}) async-start(s8[10747904]{0:T(1024)(128)(4,1)} %bitcast.32), calls=%async_computation.2 | async-start | bytes 8388608
  124.9 9.6 %slice-start.2 = ((s8[10747904]{0:T(1024)(128)(4,1)}), s8[2359296]{0:T(1024)(128)(4,1)S(1)}, s32[]{:S(2)}) async-start(s8[10747904]{0:T(1024)(128)(4,1)} %bitcast.32), calls=%async_computation.3 | async-start | bytes 4718592
  127.7 16.6 %collective-permute-start.15 = (bf16[128,1280]{1,0:T(8,128)(2,1)S(1)}, bf16[128,1280]{1,0:T(8,128)(2,1)S(1)}, u32[]{:S(2)}, u32[]{:S(2)}) collective-permute-start(bf16[128,1280]{1,0:T(8,128)(2,1)S(1)} %get-tuple-element.52), channel_id=1, source_target_pairs={{0,16},{16,32},{32,48},{48,0},{1,17},{17,33},{33,49},{49,1},{2,18}... | collective-permute-start | bytes 983048 | tf_op jit(solution)/shard_map/ppermute | solution.py:435
  129.4 12.4 %collective-permute-start.18 = (bf16[128,128]{1,0:T(8,128)(2,1)S(1)}, bf16[128,128]{1,0:T(8,128)(2,1)S(1)}, u32[]{:S(2)}, u32[]{:S(2)}) collective-permute-start(bf16[128,128]{1,0:T(8,128)(2,1)S(1)} %get-tuple-element.76), channel_id=1, source_target_pairs={{0,16},{16,32},{32,48},{48,0},{1,17},{17,33},{33,49},{49,1},{2,18}... | collective-permute-start | bytes 98312 | tf_op jit(solution)/shard_map/ppermute | solution.py:401
  130.7 14.0 %collective-permute-start.16 = (bf16[128,1280]{1,0:T(8,128)(2,1)S(1)}, bf16[128,1280]{1,0:T(8,128)(2,1)S(1)}, u32[]{:S(2)}, u32[]{:S(2)}) collective-permute-start(bf16[128,1280]{1,0:T(8,128)(2,1)S(1)} %get-tuple-element.53), channel_id=1, source_target_pairs={{0,32},{16,48},{32,0},{48,16},{1,33},{17,49},{33,1},{49,17},{2,34}... | collective-permute-start | bytes 983048 | tf_op jit(solution)/shard_map/ppermute | solution.py:435
  132.6 17.0 %collective-permute-start.17 = (bf16[128,1280]{1,0:T(8,128)(2,1)S(1)}, bf16[128,1280]{1,0:T(8,128)(2,1)S(1)}, u32[]{:S(2)}, u32[]{:S(2)}) collective-permute-start(bf16[128,1280]{1,0:T(8,128)(2,1)S(1)} %get-tuple-element.54), channel_id=1, source_target_pairs={{0,48},{16,0},{32,16},{48,32},{1,49},{17,1},{33,17},{49,33},{2,50}... | collective-permute-start | bytes 983048 | tf_op jit(solution)/shard_map/ppermute | solution.py:435
  141.8 18.6 %collective-permute-start.12 = (bf16[128,1280]{1,0:T(8,128)(2,1)S(1)}, bf16[128,1280]{1,0:T(8,128)(2,1)S(1)}, u32[]{:S(2)}, u32[]{:S(2)}) collective-permute-start(bf16[128,1280]{1,0:T(8,128)(2,1)S(1)} %get-tuple-element.48), channel_id=1, source_target_pairs={{0,16},{16,32},{32,48},{48,0},{1,17},{17,33},{33,49},{49,1},{2,18}... | collective-permute-start | bytes 983048 | tf_op jit(solution)/shard_map/ppermute | solution.py:435
  141.8 18.6 %collective-permute-start.13 = (bf16[128,1280]{1,0:T(8,128)(2,1)S(1)}, bf16[128,1280]{1,0:T(8,128)(2,1)S(1)}, u32[]{:S(2)}, u32[]{:S(2)}) collective-permute-start(bf16[128,1280]{1,0:T(8,128)(2,1)S(1)} %get-tuple-element.49), channel_id=1, source_target_pairs={{0,32},{16,48},{32,0},{48,16},{1,33},{17,49},{33,1},{49,17},{2,34}... | collective-permute-start | bytes 983048 | tf_op jit(solution)/shard_map/ppermute | solution.py:435
  144.3 16.2 %collective-permute-start.14 = (bf16[128,1280]{1,0:T(8,128)(2,1)S(1)}, bf16[128,1280]{1,0:T(8,128)(2,1)S(1)}, u32[]{:S(2)}, u32[]{:S(2)}) collective-permute-start(bf16[128,1280]{1,0:T(8,128)(2,1)S(1)} %get-tuple-element.50), channel_id=1, source_target_pairs={{0,48},{16,0},{32,16},{48,32},{1,49},{17,1},{33,17},{49,33},{2,50}... | collective-permute-start | bytes 983048 | tf_op jit(solution)/shard_map/ppermute | solution.py:435
  144.7 13.4 %collective-permute-start.19 = (bf16[128,128]{1,0:T(8,128)(2,1)S(1)}, bf16[128,128]{1,0:T(8,128)(2,1)S(1)}, u32[]{:S(2)}, u32[]{:S(2)}) collective-permute-start(bf16[128,128]{1,0:T(8,128)(2,1)S(1)} %get-tuple-element.77), channel_id=1, source_target_pairs={{0,32},{16,48},{32,0},{48,16},{1,33},{17,49},{33,1},{49,17},{2,34}... | collective-permute-start | bytes 98312 | tf_op jit(solution)/shard_map/ppermute | solution.py:401
  149.6 10.8 %collective-permute-start.20 = (bf16[128,128]{1,0:T(8,128)(2,1)S(1)}, bf16[128,128]{1,0:T(8,128)(2,1)S(1)}, u32[]{:S(2)}, u32[]{:S(2)}) collective-permute-start(bf16[128,128]{1,0:T(8,128)(2,1)S(1)} %get-tuple-element.75), channel_id=1, source_target_pairs={{0,48},{16,0},{32,16},{48,32},{1,49},{17,1},{33,17},{49,33},{2,50}... | collective-permute-start | bytes 98312 | tf_op jit(solution)/shard_map/ppermute | solution.py:401
  160.4 14.1 %copy-start.1 = (f32[32,2,5120]{2,1,0:T(2,128)S(1)}, f32[32,2,5120]{2,1,0:T(2,128)}, u32[]{:S(2)}) copy-start(f32[32,2,5120]{2,1,0:T(2,128)} %param.19) | copy-start | bytes 3932164
  166.0 3.4 %collective-permute-start.21 = (bf16[128,64]{1,0:T(8,128)(2,1)S(1)}, bf16[128,64]{1,0:T(8,128)(2,1)S(1)}, u32[]{:S(2)}, u32[]{:S(2)}) collective-permute-start(bf16[128,64]{1,0:T(8,128)(2,1)S(1)} %get-tuple-element.59), channel_id=1, source_target_pairs={{0,48},{16,0},{32,16},{48,32},{1,49},{17,1},{33,17},{49,33},{2,50}... | collective-permute-start | bytes 49160 | tf_op jit(solution)/shard_map/ppermute | solution.py:442
  168.4 4.3 %collective-permute-start.22 = (bf16[128,64]{1,0:T(8,128)(2,1)S(1)}, bf16[128,64]{1,0:T(8,128)(2,1)S(1)}, u32[]{:S(2)}, u32[]{:S(2)}) collective-permute-start(bf16[128,64]{1,0:T(8,128)(2,1)S(1)} %get-tuple-element.60), channel_id=1, source_target_pairs={{0,32},{16,48},{32,0},{48,16},{1,33},{17,49},{33,1},{49,17},{2,34}... | collective-permute-start | bytes 49160 | tf_op jit(solution)/shard_map/ppermute | solution.py:442
  169.2 4.4 %collective-permute-start.23 = (bf16[128,64]{1,0:T(8,128)(2,1)S(1)}, bf16[128,64]{1,0:T(8,128)(2,1)S(1)}, u32[]{:S(2)}, u32[]{:S(2)}) collective-permute-start(bf16[128,64]{1,0:T(8,128)(2,1)S(1)} %get-tuple-element.61), channel_id=1, source_target_pairs={{0,16},{16,32},{32,48},{48,0},{1,17},{17,33},{33,49},{49,1},{2,18}... | collective-permute-start | bytes 49160 | tf_op jit(solution)/shard_map/ppermute | solution.py:442
  (12 other events, 41.4 us)
Sparse Core Ops, SparseCore 0:
  10.6 82.0 all-gather.1
where the time goes:
time: 182 us; the launch traced here: 181 us
  Pallas kernels  94.2 us (52%)
  starting transfers between devices  32 us (18%)
  waiting for transfers between devices  21.4 us (12%)
  between operations  15 us (8%)
  local copies, waits for them, and re-layouts  14.4 us (8%)
  other arithmetic  4.43 us (2%)
    pallas_call x5, Pallas kernels, project(): pl.pallas_call(project_kernel, grid=(count // tile,), in_specs=[pl.BlockS...  38 us
    pallas_call x2, Pallas kernels, attend(): pl.pallas_call(attend_kernel, grid_spec=pltpu.PrefetchScalarGridSpec(num_...  27.3 us
    pallas_call x4, Pallas kernels, teach(): pl.pallas_call(functools.partial(teach_kernel, groups, feats, width, carr...  19.2 us
    ppermute x12, starting transfers between devices, shards(): lax.ppermute(blocks[d], 'z', along('z', z_count, d))  15.4 us
    unnamed x39, local copies, waits for them, and re-layouts  12.7 us
    pallas_call x4, Pallas kernels, combine(): pl.pallas_call(functools.partial(combine_kernel, groups), grid_spec=pltpu...  9.51 us
    ppermute x12, waiting for transfers between devices, shards(): lax.ppermute(blocks[d], 'z', along('z', z_count, d))  8.27 us
    ppermute x3, starting transfers between devices, shards(): lax.ppermute(tags[d], 'z', along('z', z_count, d))  7.41 us
  transfers between devices with their start and end apart: 25, of which 9 were waited for; matrix products, arithmetic and copies ran while one was open for 2% of the time, Pallas kernels for 49%

commit v1 on v0

--- a/solution.py
+++ b/solution.py
@@ -10,7 +10,8 @@
 from jax.sharding import PartitionSpec as P
 
 HEAD_DIM = 128
-CHUNKS = 4
+TILE = 640
+PIECES = (1920, 1920, 1280)
 HEAD_GROUP = 5
 SCALE2 = HEAD_DIM ** (-0.5) * math.log2(math.e)
 NT = (((1,), (1,)), ((), ()))
@@ -37,140 +38,196 @@
     return pl.CostEstimate(flops=flops, bytes_accessed=moved, transcendentals=0)
 
 
-def attend_kernel(info, q_ref, k_ref, v_ref, ke_ref, ve_ref, *refs):
-    o_ref = refs[-1]
-    later = info[1] == 1
-
-    @pl.when(later)
-    def both():
+def after(x, *earlier):
+    def kernel(*refs):
+        pass
+
+    anywhere = pl.BlockSpec(memory_space=pl.ANY)
+    return pl.pallas_call(
+        kernel,
+        in_specs=[anywhere] * (1 + len(earlier)),
+        out_specs=anywhere,
+        out_shape=jax.ShapeDtypeStruct(x.shape, x.dtype),
+        input_output_aliases={0: 0},
+        name="after",
+    )(x, *earlier)
+
+
+def attend_own_kernel(q_ref, k_ref, v_ref, o_ref, stat_ref):
+    for h in range(HEAD_GROUP):
+        cols = slice(h * HEAD_DIM, (h + 1) * HEAD_DIM)
+        scores = dot_nt(q_ref[:, cols], k_ref[:, cols])
+        peak = jnp.max(scores, axis=1, keepdims=True)
+        weights = jnp.exp2((scores - peak) * SCALE2)
+        total = jnp.sum(weights, axis=1, keepdims=True)
+        acc = dot_nn(weights.astype(BF16), v_ref[:, cols])
+        o_ref[:, cols] = (acc / total).astype(BF16)
+        stat_ref[:, cols] = jnp.broadcast_to(peak * SCALE2 + jnp.log2(total), acc.shape)
+
+
+def attend_own(queries, keys, values):
+    tok, width = queries.shape
+    wide = HEAD_GROUP * HEAD_DIM
+    block = pl.BlockSpec((tok, wide), lambda i: (0, i))
+    return pl.pallas_call(
+        attend_own_kernel,
+        grid=(width // wide,),
+        in_specs=[block] * 3,
+        out_specs=[block] * 2,
+        out_shape=[
+            jax.ShapeDtypeStruct((tok, width), BF16),
+            jax.ShapeDtypeStruct((tok, width), F32),
+        ],
+        compiler_params=params(56),
+        cost_estimate=cost(8 * tok * tok * width, 4 * tok * width * 2),
+        name="attend_own",
+    )(queries, keys, values)
+
+
+def attend_early_kernel(info, q_ref, k_ref, v_ref, own_ref, stat_ref, o_ref):
+    @pl.when(info[0] == 0)
+    def keep():
+        o_ref[...] = own_ref[...]
+
+    @pl.when(info[0] == 1)
+    def merge():
         for h in range(HEAD_GROUP):
             cols = slice(h * HEAD_DIM, (h + 1) * HEAD_DIM)
-            q = q_ref[:, cols]
-            s_own = dot_nt(q, k_ref[:, cols])
-            s_early = dot_nt(q, ke_ref[:, cols])
-            peak = jnp.maximum(
-                jnp.max(s_own, axis=1, keepdims=True), jnp.max(s_early, axis=1, keepdims=True)
-            )
-            p_own = jnp.exp2((s_own - peak) * SCALE2)
-            p_early = jnp.exp2((s_early - peak) * SCALE2)
-            total = jnp.sum(p_own, axis=1, keepdims=True) + jnp.sum(p_early, axis=1, keepdims=True)
-            acc = dot_nn(p_own.astype(BF16), v_ref[:, cols]) + dot_nn(
-                p_early.astype(BF16), ve_ref[:, cols]
-            )
-            o_ref[:, cols] = (acc / total).astype(BF16)
-
-    @pl.when(jnp.logical_not(later))
-    def own():
-        for h in range(HEAD_GROUP):
-            cols = slice(h * HEAD_DIM, (h + 1) * HEAD_DIM)
-            s_own = dot_nt(q_ref[:, cols], k_ref[:, cols])
-            peak = jnp.max(s_own, axis=1, keepdims=True)
-            p_own = jnp.exp2((s_own - peak) * SCALE2)
-            total = jnp.sum(p_own, axis=1, keepdims=True)
-            acc = dot_nn(p_own.astype(BF16), v_ref[:, cols])
-            o_ref[:, cols] = (acc / total).astype(BF16)
-
-
-def attend(half, frame, queries, keys, values, keys_early, values_early, earlier=()):
+            scores = dot_nt(q_ref[:, cols], k_ref[:, cols])
+            peak = jnp.max(scores, axis=1, keepdims=True)
+            weights = jnp.exp2((scores - peak) * SCALE2)
+            total = jnp.sum(weights, axis=1, keepdims=True)
+            acc = dot_nn(weights.astype(BF16), v_ref[:, cols])
+            gap = stat_ref[:, cols] - (peak * SCALE2 + jnp.log2(total))
+            share_own = 1.0 / (1.0 + jnp.exp2(-gap))
+            share_early = 1.0 / (1.0 + jnp.exp2(gap))
+            merged = share_own * own_ref[:, cols].astype(F32) + (share_early / total) * acc
+            o_ref[:, cols] = merged.astype(BF16)
+
+
+def attend_early(frame, queries, keys, values, own, stats):
     tok, width = queries.shape
-    rows = tok // 2
     wide = HEAD_GROUP * HEAD_DIM
-    whole = pl.BlockSpec((tok, wide), lambda i, info: (0, i))
-    early = pl.BlockSpec((tok, wide), lambda i, info: (0, i * info[1]))
+    block = pl.BlockSpec((tok, wide), lambda i, info: (0, i * info[0]))
     return pl.pallas_call(
-        attend_kernel,
+        attend_early_kernel,
         grid_spec=pltpu.PrefetchScalarGridSpec(
             num_scalar_prefetch=1,
             grid=(width // wide,),
-            in_specs=[pl.BlockSpec((rows, wide), lambda i, info: (info[0], i))]
-            + [whole] * 2
-            + [early] * 2
-            + [pl.BlockSpec(memory_space=pl.ANY)] * len(earlier),
-            out_specs=pl.BlockSpec((rows, wide), lambda i, info: (0, i)),
+            in_specs=[block] * 5,
+            out_specs=block,
         ),
-        out_shape=jax.ShapeDtypeStruct((rows, width), BF16),
+        out_shape=jax.ShapeDtypeStruct((tok, width), BF16),
+        input_output_aliases={4: 0},
         compiler_params=params(56),
-        cost_estimate=cost(8 * rows * tok * width, 5 * tok * width * 2),
-        name="attend",
-    )(
-        jnp.stack([half, frame]).astype(jnp.int32),
-        queries,
-        keys,
-        values,
-        keys_early,
-        values_early,
-        *earlier,
-    )
-
-
-def project_kernel(a_ref, w_ref, *refs):
-    refs[-1][...] = dot_nn(a_ref[...], w_ref[...]).astype(BF16)
-
-
-def project(a, w, start, count, earlier=(), tile=640):
+        cost_estimate=cost(8 * tok * tok * width, 5 * tok * width * 2),
+        name="attend_early",
+    )(frame.astype(jnp.int32).reshape(1), queries, keys, values, own, stats)
+
+
+def project_kernel(counts, info, a_ref, w_ref, *refs):
+    pieces = len(counts)
+    fars, owns = refs[-2 * pieces : -pieces], refs[-pieces:]
+    rows = fars[0].shape[0]
+    tile = w_ref.shape[1]
+    product = dot_nn(a_ref[...], w_ref[...]).astype(BF16)
+    first = info[0] == 0
+    own = jnp.where(first, product[:rows], product[rows:])
+    far = jnp.where(first, product[rows:], product[:rows])
+    step = 0
+    for c, count in enumerate(counts):
+        for j in range(count // tile):
+
+            @pl.when(pl.program_id(0) == step)
+            def store():
+                owns[c][:, j * tile : (j + 1) * tile] = own
+                fars[c][:, j * tile : (j + 1) * tile] = far
+
+            step += 1
+
+
+def project(half, a, w, start, counts, earlier=(), tile=TILE):
     rows, depth = a.shape
     first = start // tile
-    return pl.pallas_call(
-        project_kernel,
-        grid=(count // tile,),
-        in_specs=[
-            pl.BlockSpec((rows, depth), lambda i: (0, 0)),
-            pl.BlockSpec((depth, tile), lambda i: (0, first + i)),
-        ]
-        + [pl.BlockSpec(memory_space=pl.ANY)] * len(earlier),
-        out_specs=pl.BlockSpec((rows, tile), lambda i: (0, i)),
-        out_shape=jax.ShapeDtypeStruct((rows, count), BF16),
+    total = sum(counts)
+    outs = [pl.BlockSpec((rows // 2, count), lambda i, s: (0, 0)) for count in counts]
+    shapes = [jax.ShapeDtypeStruct((rows // 2, count), BF16) for count in counts]
+    result = pl.pallas_call(
+        functools.partial(project_kernel, counts),
+        grid_spec=pltpu.PrefetchScalarGridSpec(
+            num_scalar_prefetch=1,
+            grid=(total // tile,),
+            in_specs=[
+                pl.BlockSpec((rows, depth), lambda i, s: (0, 0)),
+                pl.BlockSpec((depth, tile), lambda i, s: (0, first + i)),
+            ]
+            + [pl.BlockSpec(memory_space=pl.ANY)] * len(earlier),
+            out_specs=outs * 2,
+        ),
+        out_shape=shapes * 2,
         compiler_params=params(56),
-        cost_estimate=cost(2 * rows * depth * count, depth * count * 2),
+        cost_estimate=cost(2 * rows * depth * total, depth * total * 2),
         name="project",
-    )(a, w, *earlier)
-
-
-def combine_kernel(groups, level, kept_ref, got_ref, noise_ref, picker_ref, *refs):
+    )(half.astype(jnp.int32).reshape(1), a, w, *earlier)
+    return list(result[: len(counts)]), list(result[len(counts) :])
+
+
+def combine_kernel(groups, steps, tagged, level, kept_ref, got_ref, noise_ref, picker_ref, *refs):
     rows_ref, picked = refs[-1 - groups], refs[-groups:]
+    tile = kept_ref.shape[1]
+    slots = picked[0].shape[0]
     rows = (kept_ref[...].astype(F32) + got_ref[...].astype(F32)).astype(BF16)
     rows_ref[...] = rows
     s = level[0]
     noisy = ((1.0 - s) * rows.astype(F32) + s * noise_ref[...].astype(F32)).astype(BF16)
-    slots = picked[0].shape[0]
-    for d, ref in enumerate(picked):
-        ref[...] = dot_nn(picker_ref[d * slots : (d + 1) * slots, :], noisy).astype(BF16)
-
-
-def combine(level, kept, got, noise, picker, buffer, earlier, start, groups, tile=640):
+    placed = dot_nn(picker_ref[...], noisy).astype(BF16)
+    for j in range(steps):
+
+        @pl.when(pl.program_id(0) == j)
+        def store():
+            for d, ref in enumerate(picked):
+                at_rows = slice(d * slots, (d + 1) * slots)
+                ref[:, j * tile : (j + 1) * tile] = placed[at_rows]
+                if tagged and j == 0:
+                    ref[:, steps * tile :] = refs[0][at_rows, :]
+
+
+def combine(level, kept, got, noise, picker, buffer, tags, earlier, start, groups, tile=TILE):
     rows, count = got.shape
+    width = noise.shape[1]
     first = start // tile
     places = picker.shape[0]
-    slots = places // groups
+    steps = count // tile
     at = pl.BlockSpec((rows, tile), lambda i, s: (0, first + i))
     local = pl.BlockSpec((rows, tile), lambda i, s: (0, i))
-    out = pl.BlockSpec((slots, tile), lambda i, s: (0, i))
+    in_specs = [local, local, at, pl.BlockSpec((places, rows), lambda i, s: (0, 0))]
+    operands = [level, kept, got, noise, picker]
+    out_width = count
+    if tags is not None:
+        in_specs.append(pl.BlockSpec(tags.shape, lambda i, s: (0, 0)))
+        operands.append(tags)
+        out_width = count + tags.shape[1]
     rest = ([] if buffer is None else [buffer]) + list(earlier)
+    block = (places // groups, out_width)
     result = pl.pallas_call(
-        functools.partial(combine_kernel, groups),
+        functools.partial(combine_kernel, groups, steps, tags is not None),
         grid_spec=pltpu.PrefetchScalarGridSpec(
             num_scalar_prefetch=1,
-            grid=(count // tile,),
-            in_specs=[
-                at,
-                local,
-                at,
-                pl.BlockSpec((places, rows), lambda i, s: (0, 0)),
-            ]
-            + [pl.BlockSpec(memory_space=pl.ANY)] * len(rest),
-            out_specs=[at] + [out] * groups,
+            grid=(steps,),
+            in_specs=in_specs + [pl.BlockSpec(memory_space=pl.ANY)] * len(rest),
+            out_specs=[at] + [pl.BlockSpec(block, lambda i, s: (0, 0))] * groups,
         ),
-        out_shape=[jax.ShapeDtypeStruct(kept.shape, BF16)]
-        + [jax.ShapeDtypeStruct((slots, count), BF16)] * groups,
-        input_output_aliases={} if buffer is None else {5: 0},
-        compiler_params=params(),
-        cost_estimate=cost(2 * rows * places * count, rows * count * 10),
+        out_shape=[jax.ShapeDtypeStruct((rows, width), BF16)]
+        + [jax.ShapeDtypeStruct(block, BF16)] * groups,
+        input_output_aliases={} if buffer is None else {len(operands): 0},
+        compiler_params=params(50),
+        cost_estimate=cost(1024, 1024),
         name="combine",
-    )(level, kept, got, noise, picker, *rest)
+    )(*operands, *rest)
     return result[0], list(result[1:])
 
 
-def teach_kernel(groups, feats, width, first, last, *refs):
+def teach_kernel(groups, feats, width, first, last, skip, *refs):
     refs = list(refs)
     weight = refs[0]
     xs = refs[1 : 1 + groups]
@@ -179,6 +236,7 @@
     if not first:
         y_in, sq_in = refs[at : at + 2]
         at += 2
+    at += skip
     if last:
         ids = refs[at : at + groups]
         shift_ref = refs[at + groups]
@@ -262,9 +320,11 @@
                 outs[d][...] = result.astype(BF16)
 
 
-def teach(weight, xs, heads, pieces, ctx, carry, ids, start, feats, width, last, tile=640):
+def teach(
+    weight, xs, heads, pieces, ctx, carry, ids, start, count, feats, width, last, earlier, tile=TILE
+):
     groups = len(xs)
-    slots, count = xs[0].shape
+    slots = xs[0].shape[0]
     half = heads.shape[0] // 2
     first = start // tile
     rows = groups * slots + pieces.shape[0]
@@ -286,9 +346,11 @@
     if carry is not None:
         in_specs += fixed
         operands += list(carry)
+    in_specs += [pl.BlockSpec(memory_space=pl.ANY)] * len(earlier)
+    operands += list(earlier)
     scratch = []
     if last:
-        in_specs += [pl.BlockSpec((slots, 128), lambda i, *s: (0, 0))] * groups
+        in_specs += [pl.BlockSpec((slots, 128), lambda i, *s: (0, PIECES[0] // 128))] * groups
         in_specs += [pl.BlockSpec((2 * half, 128), lambda i, *s: (0, width // 128))]
         operands += [*ids, heads]
         out_specs = [pl.BlockSpec((slots, 2 * feats), lambda i, *s: (0, 0))] * groups
@@ -298,7 +360,7 @@
         out_specs = fixed
         out_shape = shapes
     return pl.pallas_call(
-        functools.partial(teach_kernel, groups, feats, width, carry is None, last),
+        functools.partial(teach_kernel, groups, feats, width, carry is None, last, len(earlier)),
         grid_spec=pltpu.PrefetchScalarGridSpec(
             num_scalar_prefetch=1,
             grid=(count // tile,),
@@ -307,8 +369,8 @@
             scratch_shapes=scratch,
         ),
         out_shape=out_shape,
-        compiler_params=params(),
-        cost_estimate=cost(4 * rows * half * count, 4 * half * count + 8 * rows * half),
+        compiler_params=params(50),
+        cost_estimate=cost(1024, 1024),
         name="teach",
     )(*operands)
 
@@ -363,10 +425,10 @@
     q, k, v = queries[0, 0], key_states[0, 0], value_states[0, 0]
     width = out_proj.shape[1]
     half_rows = q.shape[0] // 2
-    chunk = width // CHUNKS
+    starts = [sum(PIECES[:c]) for c in range(len(PIECES))]
     swap = [(0, 1), (1, 0)]
 
-    def along(axis, count, d):
+    def along(count, d):
         return [(j, (j + d) % count) for j in range(count)]
 
     k_early = lax.ppermute(k, "frame", [(0, 1)])
@@ -379,7 +441,7 @@
     extra = jnp.pad(jnp.stack(split3(shift_out), axis=1), ((0, 0), (0, 125)))
     packed = jnp.concatenate([scaled, extra], axis=1)
     mine = lax.dynamic_slice_in_dim(packed, frame * feats, feats, 0)
-    heads = lax.all_gather(mine, ("frame", "y", "xh", "xl"), axis=0, tiled=True)
+    heads_x = lax.all_gather(mine, ("xh", "xl"), axis=0, tiled=True)
     group = x_count * y_count
 
     targets = routes[0, 0, :, 0]
@@ -396,10 +458,6 @@
     picker_back = (place[:, None] == places[None, :]).astype(BF16)
     tags = jnp.where(place[None, :] == places[:, None], local.astype(F32)[None, :], 0.0)
     tags = jnp.pad(jnp.sum(tags, axis=1).astype(BF16)[:, None], ((0, 0), (0, 127)))
-    tags = tags.reshape(z_count, slots, 128)
-    ids = [tags[0]] + [
-        lax.ppermute(tags[d], "z", along("z", z_count, d)) for d in range(1, z_count)
-    ]
 
     z_from = [lax.rem(z_at - d + z_count, z_count) for d in range(z_count)]
     videos = jnp.stack([(z * y_count + y_at) * lax.axis_size("xh") + xh for z in z_from])
@@ -408,38 +466,63 @@
     pieces = jnp.pad(jnp.concatenate(split3(ctx), axis=0), ((0, 8), (0, 0)))
     level = timesteps[0].astype(F32) / 1000.0
 
-    part_far = attend(1 - xl, frame, q, k, v, k_early, v_early)
-    sent = []
-    for c in range(CHUNKS):
-        sent.append(project(part_far, out_proj, c * chunk, chunk, sent[-1:]))
-    arrived = [lax.ppermute(one, "xl", swap) for one in sent]
-    part_own = attend(xl, frame, q, k, v, k_early, v_early, sent[-1:])
-    kept = project(part_own, out_proj, 0, width)
+    attended, stats = attend_own(q, k, v)
+    attended = attend_early(frame, q, k_early, v_early, attended, stats)
+    sent, kept = project(xl, attended, out_proj, 0, PIECES[:1])
+    heads = lax.all_gather(after(heads_x, *kept), ("frame", "y"), axis=0, tiled=True)
+    far, own = project(xl, attended, out_proj, PIECES[0], PIECES[1:], sent)
+    sent, kept = sent + far, kept + own
+    arrived = [lax.ppermute(sent[0], "xl", swap), lax.ppermute(sent[1], "xl", swap)]
+    arrived.append(lax.ppermute(after(sent[2], arrived[1]), "xl", swap))
 
     student = None
     carry = None
-    done = []
-    for c in range(CHUNKS):
-        student, blocks = combine(
+    got = []
+
+    def send(c, earlier):
+        student_now, blocks = combine(
             level,
-            kept,
+            kept[c],
             arrived[c],
             noise_field[0, 0],
             picker,
             student,
-            done[c - 2 : c - 1] if c > 1 else [],
-            c * chunk,
+            tags if c == 0 else None,
+            earlier,
+            starts[c],
             z_count,
         )
-        got = [blocks[0]] + [
-            lax.ppermute(blocks[d], "z", along("z", z_count, d)) for d in range(1, z_count)
-        ]
-        carry = teach(
-            weight, got, heads, pieces, ctx, carry, ids, c * chunk, feats, width, c == CHUNKS - 1
+        got.append(
+            [blocks[0]]
+            + [lax.ppermute(blocks[d], "z", along(z_count, d)) for d in range(1, z_count)]
         )
-        done.append(carry[0])
+        return student_now
+
+    def score(c, earlier):
+        return teach(
+            weight,
+            got[c],
+            heads,
+            pieces,
+            ctx,
+            carry,
+            got[0],
+            starts[c],
+            PIECES[c],
+            feats,
+            width,
+            c == len(PIECES) - 1,
+            earlier,
+        )
+
+    student = send(0, [])
+    student = send(1, [])
+    carry = score(0, got[1][:1])
+    student = send(2, carry[:1])
+    carry = score(1, got[2][:1])
+    carry = score(2, [])
     returned = [carry[0]] + [
-        lax.ppermute(carry[d], "z", along("z", z_count, z_count - d)) for d in range(1, z_count)
+        lax.ppermute(carry[d], "z", along(z_count, z_count - d)) for d in range(1, z_count)
     ]
     guided = unpick(picker_back, returned)
     return (student[None, None], guided[None, None])

time: 182 us -> 166 us (0.912)
  starting transfers between devices: 32 us -> 22.7 us
  Pallas kernels: 94.2 us -> 87.7 us
  waiting for transfers between devices: 21.4 us -> 26.4 us
  local copies, waits for them, and re-layouts: 14.4 us -> 9.9 us
    ppermute x22 -> x15, waiting for transfers between devices: 15.4 us -> 26.4 us  [the longest x9 14.3 us: send(): lax.ppermute(blocks[d], 'z', along(z_count, d))]
    pallas_call x11 -> x9, Pallas kernels: 74.8 us -> 64 us  [the longest x2 26.8 us: project(): pl.pallas_call(functools.partial(project_kernel, counts), grid_spec=pltpu...]
    ppermute x22 -> x15, starting transfers between devices: 29.3 us -> 19.9 us  [the longest x9 15.9 us: send(): lax.ppermute(blocks[d], 'z', along(z_count, d))]
    unnamed x39 -> x29, local copies, waits for them, and re-layouts: 12.7 us -> 4.95 us
    pallas_call x4 -> x3, Pallas kernels: 19.2 us -> 23.4 us  [teach(): pl.pallas_call(functools.partial(teach_kernel, groups, feats, width, carr...]
    ppermute x1, waiting for transfers between devices: 3.75 us -> 0.01 us  [shards(): v_early = lax.ppermute(v, 'frame', [(0, 1)])]
    ppermute x1, waiting for transfers between devices: 2.23 us -> 0.01 us  [shards(): k_early = lax.ppermute(k, 'frame', [(0, 1)])]
  transfers between devices with their start and end apart: 25 -> 19, of which waited for: 9 -> 8; matrix products, arithmetic and copies ran while one was open for 2% -> 5% of each run, Pallas kernels for 49% -> 49%
where the time goes in v1:
time: 166 us; the launch traced here: 165 us
  Pallas kernels  87.7 us (53%)
  waiting for transfers between devices  26.4 us (16%)
  starting transfers between devices  22.7 us (14%)
  between operations  14.9 us (9%)
  local copies, waits for them, and re-layouts  9.9 us (6%)
  other arithmetic  3.77 us (2%)
    pallas_call x2, Pallas kernels, project(): pl.pallas_call(functools.partial(project_kernel, counts), grid_spec=pltpu...  26.8 us
    pallas_call x3, Pallas kernels, teach(): pl.pallas_call(functools.partial(teach_kernel, groups, feats, width, carr...  23.4 us
    ppermute x9, starting transfers between devices, send(): lax.ppermute(blocks[d], 'z', along(z_count, d))  15.9 us
    ppermute x9, waiting for transfers between devices, send(): lax.ppermute(blocks[d], 'z', along(z_count, d))  14.3 us
    pallas_call x1, Pallas kernels, attend_early(): pl.pallas_call(attend_early_kernel, grid_spec=pltpu.PrefetchScalarGridSpe...  13.6 us
    pallas_call x3, Pallas kernels, combine(): pl.pallas_call(functools.partial(combine_kernel, groups, steps, tags is n...  12.3 us
    pallas_call x1, Pallas kernels, attend_own(): pl.pallas_call(attend_own_kernel, grid=(width // wide,), in_specs=[block]...  11.3 us
    ppermute x1, waiting for transfers between devices, shards(): lax.ppermute(sent[1], 'xl', swap)  7.26 us
  transfers between devices with their start and end apart: 19, of which 8 were waited for; matrix products, arithmetic and copies ran while one was open for 5% of the time, Pallas kernels for 49%

profile of v1, /device:TPU:1, one launch (start us, length us, event | category | flops | bytes accessed | tf_op | source)
XLA Modules:
  0.0 165.4 jit_solution(1971175743122506775)
XLA Ops:
  7.2 1.4 collective-permute-start
  8.7 1.3 collective-permute-start.1
  10.9 1.4 fusion.1
  13.3 11.3 %attend_own.1 = (bf16[512,2560]{1,0:T(8,128)(2,1)}, f32[512,2560]{1,0:T(8,128)}) custom-call(bf16[512,2560]{1,0:T(8,128)(2,1)} %bitcast.43, bf16[512,2560]{1,0:T(8,128)(2,1)} %bitcast.40, bf16[512,2560]{1,0:T(8,128)(2,1)} %bitcast.42), custom_call_target="tpu_custom_call" | custom-call | flops 5368709120 | bytes 10485760 | tf_op jit(solution)/shard_map/attend_own/pallas_call | solution.py:72
  24.5 13.6 %attend_early.1.a_ref = bf16[512,2560]{1,0:T(8,128)(2,1)} custom-call(s32[1]{0:T(128)} %bitcast.2.info, bf16[512,2560]{1,0:T(8,128)(2,1)} %bitcast.44, bf16[512,2560]{1,0:T(8,128)(2,1)} %collective-permute-done.k_ref, bf16[512,2560]{1,0:T(8,128)(2,1)} %collective-permute-done.1.v_ref, ...), custom_call_target="tpu_custom_call", output_to_operand_aliasing={{}: (4, {})} | custom-call | flops 5368709120 | bytes 13107200 | tf_op jit(solution)/shard_map/attend_early/pallas_call | solution.py:112
  38.1 10.9 %project.2 = (bf16[256,1920]{1,0:T(8,128)(2,1)}, bf16[256,1920]{1,0:T(8,128)(2,1)}) custom-call(s32[1]{0:T(128)} %bitcast.1.info, bf16[512,2560]{1,0:T(8,128)(2,1)} %attend_early.1.a_ref, bf16[2560,5120]{1,0:T(8,128)(2,1)} %w_ref.3), custom_call_target="tpu_custom_call" | custom-call | flops 5033164800 | bytes 9830400 | tf_op jit(solution)/shard_map/project/pallas_call | solution.py:155
  49.1 2.1 %collective-permute-start.4 = (bf16[256,1920]{1,0:T(8,128)(2,1)}, bf16[256,1920]{1,0:T(8,128)(2,1)S(1)}, u32[]{:S(2)}, u32[]{:S(2)}) collective-permute-start(bf16[256,1920]{1,0:T(8,128)(2,1)} %get-tuple-element.35.refs_0_), channel_id=1, source_target_pairs={{0,1},{1,0},{2,3},{3,2},{4,5},{5,4},{6,7},{7,6},{8,9},{9,8},{10,11... | collective-permute-start | bytes 2949128 | tf_op jit(solution)/shard_map/ppermute | solution.py:475
  51.2 15.9 %project.3 = (bf16[256,1920]{1,0:T(8,128)(2,1)}, bf16[256,1280]{1,0:T(8,128)(2,1)}, bf16[256,1920]{1,0:T(8,128)(2,1)}, bf16[256,1280]{1,0:T(8,128)(2,1)}) custom-call(s32[1]{0:T(128)} %bitcast.1.info, bf16[512,2560]{1,0:T(8,128)(2,1)} %attend_early.1.a_ref, bf16[2560,5120]{1,0:T(8,128)(2,1)} %w_ref.3, bf16[256,1920]{1,0:T(8,128)(2,1)} %get-tuple-element.35.refs_0_), custom_call_target="tpu_custom_call" | custom-call | flops 8388608000 | bytes 16384000 | tf_op jit(solution)/shard_map/project/pallas_call | solution.py:155
  69.1 1.4 gather_fusion.1
  72.6 1.3 collective-permute-done.4.got_ref
  74.9 4.6 %combine.3 = (bf16[256,5120]{1,0:T(8,128)(2,1)}, bf16[128,2048]{1,0:T(8,128)(2,1)S(1)}, bf16[128,2048]{1,0:T(8,128)(2,1)}, bf16[128,2048]{1,0:T(8,128)(2,1)}, bf16[128,2048]{1,0:T(8,128)(2,1)S(1)}) custom-call(f32[1]{0:T(128)} %bitcast.level, bf16[256,1920]{1,0:T(8,128)(2,1)S(1)} %copy-done.2, bf16[256,1920]{1,0:T(8,128)(2,1)} %copy-done.12, ...), custom_call_target="tpu_custom_call" | custom-call | flops 1024 | bytes 1024 | tf_op jit(solution)/shard_map/combine/pallas_call | solution.py:212
  79.5 1.9 %collective-permute-start.5 = (bf16[128,2048]{1,0:T(8,128)(2,1)}, bf16[128,2048]{1,0:T(8,128)(2,1)S(1)}, u32[]{:S(2)}, u32[]{:S(2)}) collective-permute-start(bf16[128,2048]{1,0:T(8,128)(2,1)} %get-tuple-element.44), channel_id=1, source_target_pairs={{0,16},{16,32},{32,48},{48,0},{1,17},{17,33},{33,49},{49,1},{2,18}... | collective-permute-start | bytes 1572872 | tf_op jit(solution)/shard_map/ppermute | solution.py:497
  81.3 2.9 %collective-permute-start.6 = (bf16[128,2048]{1,0:T(8,128)(2,1)}, bf16[128,2048]{1,0:T(8,128)(2,1)S(1)}, u32[]{:S(2)}, u32[]{:S(2)}) collective-permute-start(bf16[128,2048]{1,0:T(8,128)(2,1)} %get-tuple-element.45), channel_id=1, source_target_pairs={{0,32},{16,48},{32,0},{48,16},{1,33},{17,49},{33,1},{49,17},{2,34}... | collective-permute-start | bytes 1572872 | tf_op jit(solution)/shard_map/ppermute | solution.py:497
  84.3 7.3 %collective-permute-done.2.refs_1_.got_ref = bf16[256,1920]{1,0:T(8,128)(2,1)} collective-permute-done((bf16[256,1920]{1,0:T(8,128)(2,1)}, bf16[256,1920]{1,0:T(8,128)(2,1)}, u32[]{:S(2)}, u32[]{:S(2)}) %collective-permute-start.2) | collective-permute-done | bytes 983072 | tf_op jit(solution)/shard_map/ppermute | solution.py:475
  91.9 3.2 %collective-permute-start.7 = (bf16[128,2048]{1,0:T(8,128)(2,1)S(1)}, bf16[128,2048]{1,0:T(8,128)(2,1)S(1)}, u32[]{:S(2)}, u32[]{:S(2)}) collective-permute-start(bf16[128,2048]{1,0:T(8,128)(2,1)S(1)} %get-tuple-element.46), channel_id=1, source_target_pairs={{0,48},{16,0},{32,16},{48,32},{1,49},{17,1},{33,17},{49,33},{2,50}... | collective-permute-start | bytes 1572872 | tf_op jit(solution)/shard_map/ppermute | solution.py:497
  95.0 1.2 copy-done.9
  96.2 4.7 %combine.4 = (bf16[256,5120]{1,0:T(8,128)(2,1)}, bf16[128,1920]{1,0:T(8,128)(2,1)S(1)}, bf16[128,1920]{1,0:T(8,128)(2,1)}, bf16[128,1920]{1,0:T(8,128)(2,1)}, bf16[128,1920]{1,0:T(8,128)(2,1)}) custom-call(f32[1]{0:T(128)} %bitcast.level, bf16[256,1920]{1,0:T(8,128)(2,1)S(1)} %copy-done.9, ...), custom_call_target="tpu_custom_call", output_to_operand_aliasing={{0}: (5, {})} | custom-call | flops 1024 | bytes 1024 | tf_op jit(solution)/shard_map/combine/pallas_call | solution.py:212
  101.7 1.6 collective-permute-start.12
  103.3 1.1 collective-permute-start.13
  105.1 9.3 %collective-permute-done.7.refs_4_.refs_13_ = bf16[128,2048]{1,0:T(8,128)(2,1)S(1)} collective-permute-done((bf16[128,2048]{1,0:T(8,128)(2,1)S(1)}, bf16[128,2048]{1,0:T(8,128)(2,1)S(1)}, u32[]{:S(2)}, u32[]{:S(2)}) %collective-permute-start.7) | collective-permute-done | bytes 524320 | tf_op jit(solution)/shard_map/ppermute | solution.py:497
  114.5 1.2 copy-done.7
  115.7 7.9 %teach.3 = (f32[544,1024]{1,0:T(8,128)}, f32[2,512,128]{2,1,0:T(8,128)S(1)}) custom-call(f32[4]{0:T(128)S(1)} %gather_fusion, bf16[128,2048]{1,0:T(8,128)(2,1)S(1)} %get-tuple-element.43.refs_1_.refs_10_, bf16[128,2048]{1,0:T(8,128)(2,1)S(1)} %collective-permute-done.5.refs_2_.refs_11_, bf16[128,2048]{1,0:T(8,128)(2,1)S(1)} %collective-permute-done.6.refs_3_.refs_12_, ...), custom_call_target="tpu_custom_call" | custom-call | flops 1024 | bytes 1024 | tf_op jit(solution)/shard_map/teach/pallas_call | solution.py:362
  123.6 3.1 %combine.5 = (bf16[256,5120]{1,0:T(8,128)(2,1)}, bf16[128,1280]{1,0:T(8,128)(2,1)S(1)}, bf16[128,1280]{1,0:T(8,128)(2,1)S(1)}, bf16[128,1280]{1,0:T(8,128)(2,1)S(1)}, bf16[128,1280]{1,0:T(8,128)(2,1)S(1)}) custom-call(f32[1]{0:T(128)} %bitcast.level, bf16[256,1280]{1,0:T(8,128)(2,1)S(1)} %copy-done.10, ...), custom_call_target="tpu_custom_call", output_to_operand_aliasing={{0}: (5, {})} | custom-call | flops 1024 | bytes 1024 | tf_op jit(solution)/shard_map/combine/pallas_call | solution.py:212
  126.7 4.0 %collective-permute-start.10 = (bf16[128,1280]{1,0:T(8,128)(2,1)S(1)}, bf16[128,1280]{1,0:T(8,128)(2,1)S(1)}, u32[]{:S(2)}, u32[]{:S(2)}) collective-permute-start(bf16[128,1280]{1,0:T(8,128)(2,1)S(1)} %get-tuple-element.53), channel_id=1, source_target_pairs={{0,48},{16,0},{32,16},{48,32},{1,49},{17,1},{33,17},{49,33},{2,50}... | collective-permute-start | bytes 983048 | tf_op jit(solution)/shard_map/ppermute | solution.py:497
  130.7 1.2 collective-permute-start.9
  131.9 8.4 %teach.4 = (f32[544,1024]{1,0:T(8,128)}, f32[2,512,128]{2,1,0:T(8,128)S(1)}) custom-call(f32[4]{0:T(128)S(1)} %gather_fusion, bf16[128,1920]{1,0:T(8,128)(2,1)S(1)} %copy-done.8, bf16[128,1920]{1,0:T(8,128)(2,1)} %collective-permute-done.11.refs_2_, bf16[128,1920]{1,0:T(8,128)(2,1)} %collective-permute-done.12.refs_3_, ...), custom_call_target="tpu_custom_call" | custom-call | flops 1024 | bytes 1024 | tf_op jit(solution)/shard_map/teach/pallas_call | solution.py:362
  140.3 1.5 collective-permute-done.10.refs_4_
  141.8 3.4 %collective-permute-done.8.refs_2_ = bf16[128,1280]{1,0:T(8,128)(2,1)S(1)} collective-permute-done((bf16[128,1280]{1,0:T(8,128)(2,1)S(1)}, bf16[128,1280]{1,0:T(8,128)(2,1)S(1)}, u32[]{:S(2)}, u32[]{:S(2)}) %collective-permute-start.8) | collective-permute-done | bytes 327712 | tf_op jit(solution)/shard_map/ppermute | solution.py:497
  145.2 7.2 %teach.5 = (bf16[128,64]{1,0:T(8,128)(2,1)S(1)}, bf16[128,64]{1,0:T(8,128)(2,1)S(1)}, bf16[128,64]{1,0:T(8,128)(2,1)S(1)}, bf16[128,64]{1,0:T(8,128)(2,1)S(1)}) custom-call(f32[4]{0:T(128)S(1)} %gather_fusion, bf16[128,1280]{1,0:T(8,128)(2,1)S(1)} %get-tuple-element.50.refs_10_.refs_1_, bf16[128,1280]{1,0:T(8,128)(2,1)S(1)} %collective-permute-done.8.refs_2_, ...), custom_call_target="tpu_custom_call" | custom-call | flops 1024 | bytes 1024 | tf_op jit(solution)/shard_map/teach/pallas_call | solution.py:362
  152.6 1.4 collective-permute-start.16
  154.1 1.5 collective-permute-done.14.refs_1_
  155.5 1.6 collective-permute-done.15.refs_2_
  (71 shorter events, 9.9 us)
Async XLA Ops:
  7.2 62.0 %copy-start = (f32[32,2,5120]{2,1,0:T(2,128)S(1)}, f32[32,2,5120]{2,1,0:T(2,128)}, u32[]{:S(2)}) copy-start(f32[32,2,5120]{2,1,0:T(2,128)} %param.19) | copy-start | bytes 3932164
  7.2 41.8 %all-gather.3.cloned.1.call-start = ((), (), s32[]{:S(2)}) async-start(), calls=%async_computation | async-start | bytes 1679360 | tf_op jit(solution)/shard_map/all_gather | solution.py:444
  7.2 17.3 %collective-permute-start = (bf16[512,2560]{1,0:T(8,128)(2,1)}, bf16[512,2560]{1,0:T(8,128)(2,1)}, u32[]{:S(2)}, u32[]{:S(2)}) collective-permute-start(bf16[512,2560]{1,0:T(8,128)(2,1)} %bitcast.39), channel_id=1, source_target_pairs={{0,64},{1,65},{2,66},{3,67},{4,68},{5,69},{6,70},{7,71},{8,72},{9,... | collective-permute-start | bytes 7864328 | tf_op jit(solution)/shard_map/ppermute | solution.py:434
  8.7 15.9 %collective-permute-start.1 = (bf16[512,2560]{1,0:T(8,128)(2,1)}, bf16[512,2560]{1,0:T(8,128)(2,1)}, u32[]{:S(2)}, u32[]{:S(2)}) collective-permute-start(bf16[512,2560]{1,0:T(8,128)(2,1)} %bitcast.41), channel_id=1, source_target_pairs={{0,64},{1,65},{2,66},{3,67},{4,68},{5,69},{6,70},{7,71},{8,72},{9,... | collective-permute-start | bytes 7864328 | tf_op jit(solution)/shard_map/ppermute | solution.py:435
  13.2 101.3 %all-gather.5.cloned.1.call-start = ((), (), s32[]{:S(2)}) async-start(), calls=%async_computation.1 | async-start | bytes 12091392 | tf_op jit(solution)/shard_map/all_gather | solution.py:472
  49.1 18.1 %copy-start.13 = (s32[1,1,256,1]{2,3,1,0:T(1,128)S(1)}, s32[1,1,256,1]{2,3,1,0:T(1,128)}, u32[]{:S(2)}) copy-start(s32[1,1,256,1]{2,3,1,0:T(1,128)} %param.17) | copy-start | bytes 3076
  49.1 25.8 %copy-start.2 = (bf16[256,1920]{1,0:T(8,128)(2,1)S(1)}, bf16[256,1920]{1,0:T(8,128)(2,1)}, u32[]{:S(2)}) copy-start(bf16[256,1920]{1,0:T(8,128)(2,1)} %get-tuple-element.40.kept_ref.refs_1_) | copy-start | bytes 2949124
  49.1 24.8 %collective-permute-start.4 = (bf16[256,1920]{1,0:T(8,128)(2,1)}, bf16[256,1920]{1,0:T(8,128)(2,1)S(1)}, u32[]{:S(2)}, u32[]{:S(2)}) collective-permute-start(bf16[256,1920]{1,0:T(8,128)(2,1)} %get-tuple-element.35.refs_0_), channel_id=1, source_target_pairs={{0,1},{1,0},{2,3},{3,2},{4,5},{5,4},{6,7},{7,6},{8,9},{9,8},{10,11... | collective-permute-start | bytes 2949128 | tf_op jit(solution)/shard_map/ppermute | solution.py:475
  67.1 24.4 %collective-permute-start.2 = (bf16[256,1920]{1,0:T(8,128)(2,1)}, bf16[256,1920]{1,0:T(8,128)(2,1)}, u32[]{:S(2)}, u32[]{:S(2)}) collective-permute-start(bf16[256,1920]{1,0:T(8,128)(2,1)} %get-tuple-element.38), channel_id=1, source_target_pairs={{0,1},{1,0},{2,3},{3,2},{4,5},{5,4},{6,7},{7,6},{8,9},{9,8},{10,11... | collective-permute-start | bytes 2949128 | tf_op jit(solution)/shard_map/ppermute | solution.py:475
  73.9 1.0 copy-start.12
  79.5 22.2 %collective-permute-start.5 = (bf16[128,2048]{1,0:T(8,128)(2,1)}, bf16[128,2048]{1,0:T(8,128)(2,1)S(1)}, u32[]{:S(2)}, u32[]{:S(2)}) collective-permute-start(bf16[128,2048]{1,0:T(8,128)(2,1)} %get-tuple-element.44), channel_id=1, source_target_pairs={{0,16},{16,32},{32,48},{48,0},{1,17},{17,33},{33,49},{49,1},{2,18}... | collective-permute-start | bytes 1572872 | tf_op jit(solution)/shard_map/ppermute | solution.py:497
  81.3 22.0 %collective-permute-start.6 = (bf16[128,2048]{1,0:T(8,128)(2,1)}, bf16[128,2048]{1,0:T(8,128)(2,1)S(1)}, u32[]{:S(2)}, u32[]{:S(2)}) collective-permute-start(bf16[128,2048]{1,0:T(8,128)(2,1)} %get-tuple-element.45), channel_id=1, source_target_pairs={{0,32},{16,48},{32,0},{48,16},{1,33},{17,49},{33,1},{49,17},{2,34}... | collective-permute-start | bytes 1572872 | tf_op jit(solution)/shard_map/ppermute | solution.py:497
  91.5 32.0 %collective-permute-start.3 = (bf16[256,1280]{1,0:T(8,128)(2,1)}, bf16[256,1280]{1,0:T(8,128)(2,1)}, u32[]{:S(2)}, u32[]{:S(2)}) collective-permute-start(bf16[256,1280]{1,0:T(8,128)(2,1)} %after.2), channel_id=1, source_target_pairs={{0,1},{1,0},{2,3},{3,2},{4,5},{5,4},{6,7},{7,6},{8,9},{9,8},{10,11... | collective-permute-start | bytes 1966088 | tf_op jit(solution)/shard_map/ppermute | solution.py:476
  91.9 22.6 %collective-permute-start.7 = (bf16[128,2048]{1,0:T(8,128)(2,1)S(1)}, bf16[128,2048]{1,0:T(8,128)(2,1)S(1)}, u32[]{:S(2)}, u32[]{:S(2)}) collective-permute-start(bf16[128,2048]{1,0:T(8,128)(2,1)S(1)} %get-tuple-element.46), channel_id=1, source_target_pairs={{0,48},{16,0},{32,16},{48,32},{1,49},{17,1},{33,17},{49,33},{2,50}... | collective-permute-start | bytes 1572872 | tf_op jit(solution)/shard_map/ppermute | solution.py:497
  95.0 1.2 copy-start.9
  96.2 8.3 %copy-start.11 = (f32[32]{0:T(128)S(1)}, f32[32]{0:T(128)}, u32[]{:S(2)}) copy-start(f32[32]{0:T(128)} %param.20) | copy-start | bytes 388
  101.7 29.0 %collective-permute-start.11 = (bf16[128,1920]{1,0:T(8,128)(2,1)}, bf16[128,1920]{1,0:T(8,128)(2,1)}, u32[]{:S(2)}, u32[]{:S(2)}) collective-permute-start(bf16[128,1920]{1,0:T(8,128)(2,1)} %get-tuple-element.54), channel_id=1, source_target_pairs={{0,16},{16,32},{32,48},{48,0},{1,17},{17,33},{33,49},{49,1},{2,18}... | collective-permute-start | bytes 1474568 | tf_op jit(solution)/shard_map/ppermute | solution.py:497
  101.7 30.2 %collective-permute-start.12 = (bf16[128,1920]{1,0:T(8,128)(2,1)}, bf16[128,1920]{1,0:T(8,128)(2,1)}, u32[]{:S(2)}, u32[]{:S(2)}) collective-permute-start(bf16[128,1920]{1,0:T(8,128)(2,1)} %get-tuple-element.55), channel_id=1, source_target_pairs={{0,32},{16,48},{32,0},{48,16},{1,33},{17,49},{33,1},{49,17},{2,34}... | collective-permute-start | bytes 1474568 | tf_op jit(solution)/shard_map/ppermute | solution.py:497
  103.3 20.2 %copy-start.3 = (bf16[128,2048]{1,0:T(8,128)(2,1)}, bf16[128,2048]{1,0:T(8,128)(2,1)S(1)}, u32[]{:S(2)}) copy-start(bf16[128,2048]{1,0:T(8,128)(2,1)S(1)} %collective-permute-done.6.refs_3_.refs_12_) | copy-start | bytes 1572868
  103.3 28.5 %collective-permute-start.13 = (bf16[128,1920]{1,0:T(8,128)(2,1)}, bf16[128,1920]{1,0:T(8,128)(2,1)}, u32[]{:S(2)}, u32[]{:S(2)}) collective-permute-start(bf16[128,1920]{1,0:T(8,128)(2,1)} %get-tuple-element.56), channel_id=1, source_target_pairs={{0,48},{16,0},{32,16},{48,32},{1,49},{17,1},{33,17},{49,33},{2,50}... | collective-permute-start | bytes 1474568 | tf_op jit(solution)/shard_map/ppermute | solution.py:497
  114.5 9.1 %copy-start.5 = (bf16[128,2048]{1,0:T(8,128)(2,1)}, bf16[128,2048]{1,0:T(8,128)(2,1)S(1)}, u32[]{:S(2)}) copy-start(bf16[128,2048]{1,0:T(8,128)(2,1)S(1)} %collective-permute-done.7.refs_4_.refs_13_) | copy-start | bytes 1572868
  114.5 1.2 copy-start.7
  115.7 7.9 %copy-start.10 = (bf16[256,1280]{1,0:T(8,128)(2,1)S(1)}, bf16[256,1280]{1,0:T(8,128)(2,1)}, u32[]{:S(2)}) copy-start(bf16[256,1280]{1,0:T(8,128)(2,1)} %get-tuple-element.36.kept_ref) | copy-start | bytes 1966084
  123.6 8.3 %copy-start.8 = (bf16[128,1920]{1,0:T(8,128)(2,1)S(1)}, bf16[128,1920]{1,0:T(8,128)(2,1)}, u32[]{:S(2)}) copy-start(bf16[128,1920]{1,0:T(8,128)(2,1)} %copy-done.6) | copy-start | bytes 1474564
  126.7 15.2 %collective-permute-start.10 = (bf16[128,1280]{1,0:T(8,128)(2,1)S(1)}, bf16[128,1280]{1,0:T(8,128)(2,1)S(1)}, u32[]{:S(2)}, u32[]{:S(2)}) collective-permute-start(bf16[128,1280]{1,0:T(8,128)(2,1)S(1)} %get-tuple-element.53), channel_id=1, source_target_pairs={{0,48},{16,0},{32,16},{48,32},{1,49},{17,1},{33,17},{49,33},{2,50}... | collective-permute-start | bytes 983048 | tf_op jit(solution)/shard_map/ppermute | solution.py:497
  130.7 14.6 %collective-permute-start.8 = (bf16[128,1280]{1,0:T(8,128)(2,1)S(1)}, bf16[128,1280]{1,0:T(8,128)(2,1)S(1)}, u32[]{:S(2)}, u32[]{:S(2)}) collective-permute-start(bf16[128,1280]{1,0:T(8,128)(2,1)S(1)} %get-tuple-element.51), channel_id=1, source_target_pairs={{0,16},{16,32},{32,48},{48,0},{1,17},{17,33},{33,49},{49,1},{2,18}... | collective-permute-start | bytes 983048 | tf_op jit(solution)/shard_map/ppermute | solution.py:497
  130.7 14.6 %collective-permute-start.9 = (bf16[128,1280]{1,0:T(8,128)(2,1)S(1)}, bf16[128,1280]{1,0:T(8,128)(2,1)S(1)}, u32[]{:S(2)}, u32[]{:S(2)}) collective-permute-start(bf16[128,1280]{1,0:T(8,128)(2,1)S(1)} %get-tuple-element.52), channel_id=1, source_target_pairs={{0,32},{16,48},{32,0},{48,16},{1,33},{17,49},{33,1},{49,17},{2,34}... | collective-permute-start | bytes 983048 | tf_op jit(solution)/shard_map/ppermute | solution.py:497
  131.9 13.4 %copy-start.4 = (bf16[128,2048]{1,0:T(8,128)(2,1)S(1)}, bf16[128,2048]{1,0:T(8,128)(2,1)}, u32[]{:S(2)}) copy-start(bf16[128,2048]{1,0:T(8,128)(2,1)} %copy-done.3) | copy-start | bytes 1572868
  145.2 13.3 %copy-start.1 = (f32[32,2,5120]{2,1,0:T(2,128)S(1)}, f32[32,2,5120]{2,1,0:T(2,128)}, u32[]{:S(2)}) copy-start(f32[32,2,5120]{2,1,0:T(2,128)} %param.19) | copy-start | bytes 3932164
  152.4 3.1 %collective-permute-start.14 = (bf16[128,64]{1,0:T(8,128)(2,1)S(1)}, bf16[128,64]{1,0:T(8,128)(2,1)S(1)}, u32[]{:S(2)}, u32[]{:S(2)}) collective-permute-start(bf16[128,64]{1,0:T(8,128)(2,1)S(1)} %get-tuple-element.61), channel_id=1, source_target_pairs={{0,48},{16,0},{32,16},{48,32},{1,49},{17,1},{33,17},{49,33},{2,50}... | collective-permute-start | bytes 49160 | tf_op jit(solution)/shard_map/ppermute | solution.py:525
  152.5 4.6 %collective-permute-start.15 = (bf16[128,64]{1,0:T(8,128)(2,1)S(1)}, bf16[128,64]{1,0:T(8,128)(2,1)S(1)}, u32[]{:S(2)}, u32[]{:S(2)}) collective-permute-start(bf16[128,64]{1,0:T(8,128)(2,1)S(1)} %get-tuple-element.62), channel_id=1, source_target_pairs={{0,32},{16,48},{32,0},{48,16},{1,33},{17,49},{33,1},{49,17},{2,34}... | collective-permute-start | bytes 49160 | tf_op jit(solution)/shard_map/ppermute | solution.py:525
  152.6 5.1 %collective-permute-start.16 = (bf16[128,64]{1,0:T(8,128)(2,1)S(1)}, bf16[128,64]{1,0:T(8,128)(2,1)S(1)}, u32[]{:S(2)}, u32[]{:S(2)}) collective-permute-start(bf16[128,64]{1,0:T(8,128)(2,1)S(1)} %get-tuple-element.63), channel_id=1, source_target_pairs={{0,16},{16,32},{32,48},{48,0},{1,17},{17,33},{33,49},{49,1},{2,18}... | collective-permute-start | bytes 49160 | tf_op jit(solution)/shard_map/ppermute | solution.py:525
  (1 other events, 0.8 us)
Sparse Core Ops, SparseCore 0:
  13.3 30.8 all-gather.2
  49.2 62.6 all-gather.4

commit v2 on v1

--- a/solution.py
+++ b/solution.py
@@ -517,9 +517,9 @@
 
     student = send(0, [])
     student = send(1, [])
-    carry = score(0, got[1][:1])
-    student = send(2, carry[:1])
-    carry = score(1, got[2][:1])
+    student = send(2, got[0][1:])
+    carry = score(0, got[2][:1])
+    carry = score(1, [])
     carry = score(2, [])
     returned = [carry[0]] + [
         lax.ppermute(carry[d], "z", along(z_count, z_count - d)) for d in range(1, z_count)

time: 166 us -> 162 us (0.976)
  waiting for transfers between devices: 26.4 us -> 15.7 us
  starting transfers between devices: 22.7 us -> 30.5 us
  local copies, waits for them, and re-layouts: 9.9 us -> 7.3 us
    ppermute x9, waiting for transfers between devices: 14.3 us -> 0.28 us  [send(): lax.ppermute(blocks[d], 'z', along(z_count, d))]
    ppermute x9, starting transfers between devices: 15.9 us -> 22.8 us  [send(): lax.ppermute(blocks[d], 'z', along(z_count, d))]
    ppermute x1, waiting for transfers between devices: 1.28 us -> 4.4 us  [shards(): lax.ppermute(sent[0], 'xl', swap)]
    unnamed x29 -> x39, local copies, waits for them, and re-layouts: 4.95 us -> 5.54 us
  transfers between devices with their start and end apart: 19 -> 19, of which waited for: 8 -> 7; matrix products, arithmetic and copies ran while one was open for 5% -> 4% of each run, Pallas kernels for 49% -> 50%
where the time goes in v2:
time: 162 us; the launch traced here: 161 us
  Pallas kernels  88.1 us (54%)
  starting transfers between devices  30.5 us (19%)
  waiting for transfers between devices  15.7 us (10%)
  between operations  15 us (9%)
  local copies, waits for them, and re-layouts  7.3 us (5%)
  other arithmetic  4.4 us (3%)
    pallas_call x2, Pallas kernels, project(): pl.pallas_call(functools.partial(project_kernel, counts), grid_spec=pltpu...  26.9 us
    pallas_call x3, Pallas kernels, teach(): pl.pallas_call(functools.partial(teach_kernel, groups, feats, width, carr...  23.6 us
    ppermute x9, starting transfers between devices, send(): lax.ppermute(blocks[d], 'z', along(z_count, d))  22.8 us
    pallas_call x1, Pallas kernels, attend_early(): pl.pallas_call(attend_early_kernel, grid_spec=pltpu.PrefetchScalarGridSpe...  13.6 us
    pallas_call x3, Pallas kernels, combine(): pl.pallas_call(functools.partial(combine_kernel, groups, steps, tags is n...  12.6 us
    pallas_call x1, Pallas kernels, attend_own(): pl.pallas_call(attend_own_kernel, grid=(width // wide,), in_specs=[block]...  11.3 us
    ppermute x1, waiting for transfers between devices, shards(): lax.ppermute(sent[1], 'xl', swap)  6.86 us
    unnamed x39, local copies, waits for them, and re-layouts  5.54 us
  transfers between devices with their start and end apart: 19, of which 7 were waited for; matrix products, arithmetic and copies ran while one was open for 4% of the time, Pallas kernels for 50%

profile of v2, /device:TPU:1, one launch (start us, length us, event | category | flops | bytes accessed | tf_op | source)
XLA Modules:
  0.0 161.1 jit_solution(1946139264481911738)
XLA Ops:
  7.2 1.4 collective-permute-start
  8.7 1.3 collective-permute-start.1
  10.0 0.9 fusion.21
  10.9 1.4 fusion.1
  13.3 11.3 %attend_own.1 = (bf16[512,2560]{1,0:T(8,128)(2,1)}, f32[512,2560]{1,0:T(8,128)}) custom-call(bf16[512,2560]{1,0:T(8,128)(2,1)} %bitcast.43, bf16[512,2560]{1,0:T(8,128)(2,1)} %bitcast.40, bf16[512,2560]{1,0:T(8,128)(2,1)} %bitcast.42), custom_call_target="tpu_custom_call" | custom-call | flops 5368709120 | bytes 10485760 | tf_op jit(solution)/shard_map/attend_own/pallas_call | solution.py:72
  24.5 13.6 %attend_early.1.a_ref = bf16[512,2560]{1,0:T(8,128)(2,1)} custom-call(s32[1]{0:T(128)} %bitcast.2.info, bf16[512,2560]{1,0:T(8,128)(2,1)} %bitcast.44, bf16[512,2560]{1,0:T(8,128)(2,1)} %collective-permute-done.k_ref, bf16[512,2560]{1,0:T(8,128)(2,1)} %collective-permute-done.1.v_ref, ...), custom_call_target="tpu_custom_call", output_to_operand_aliasing={{}: (4, {})} | custom-call | flops 5368709120 | bytes 13107200 | tf_op jit(solution)/shard_map/attend_early/pallas_call | solution.py:112
  38.1 10.9 %project.2 = (bf16[256,1920]{1,0:T(8,128)(2,1)}, bf16[256,1920]{1,0:T(8,128)(2,1)}) custom-call(s32[1]{0:T(128)} %bitcast.1.info, bf16[512,2560]{1,0:T(8,128)(2,1)} %attend_early.1.a_ref, bf16[2560,5120]{1,0:T(8,128)(2,1)} %w_ref.3), custom_call_target="tpu_custom_call" | custom-call | flops 5033164800 | bytes 9830400 | tf_op jit(solution)/shard_map/project/pallas_call | solution.py:155
  49.1 2.1 %collective-permute-start.4 = (bf16[256,1920]{1,0:T(8,128)(2,1)}, bf16[256,1920]{1,0:T(8,128)(2,1)}, u32[]{:S(2)}, u32[]{:S(2)}) collective-permute-start(bf16[256,1920]{1,0:T(8,128)(2,1)} %get-tuple-element.35.refs_0_), channel_id=1, source_target_pairs={{0,1},{1,0},{2,3},{3,2},{4,5},{5,4},{6,7},{7,6},{8,9},{9,8},{10,11... | collective-permute-start | bytes 2949128 | tf_op jit(solution)/shard_map/ppermute | solution.py:475
  51.2 16.0 %project.3 = (bf16[256,1920]{1,0:T(8,128)(2,1)}, bf16[256,1280]{1,0:T(8,128)(2,1)}, bf16[256,1920]{1,0:T(8,128)(2,1)}, bf16[256,1280]{1,0:T(8,128)(2,1)}) custom-call(s32[1]{0:T(128)} %bitcast.1.info, bf16[512,2560]{1,0:T(8,128)(2,1)} %attend_early.1.a_ref, bf16[2560,5120]{1,0:T(8,128)(2,1)} %w_ref.3, bf16[256,1920]{1,0:T(8,128)(2,1)} %get-tuple-element.35.refs_0_), custom_call_target="tpu_custom_call" | custom-call | flops 8388608000 | bytes 16384000 | tf_op jit(solution)/shard_map/project/pallas_call | solution.py:155
  69.5 4.4 %collective-permute-done.4.got_ref = bf16[256,1920]{1,0:T(8,128)(2,1)} collective-permute-done((bf16[256,1920]{1,0:T(8,128)(2,1)}, bf16[256,1920]{1,0:T(8,128)(2,1)}, u32[]{:S(2)}, u32[]{:S(2)}) %collective-permute-start.4) | collective-permute-done | bytes 983072 | tf_op jit(solution)/shard_map/ppermute | solution.py:475
  73.9 4.9 %combine.3 = (bf16[256,5120]{1,0:T(8,128)(2,1)}, bf16[128,2048]{1,0:T(8,128)(2,1)S(1)}, bf16[128,2048]{1,0:T(8,128)(2,1)}, bf16[128,2048]{1,0:T(8,128)(2,1)}, bf16[128,2048]{1,0:T(8,128)(2,1)}) custom-call(f32[1]{0:T(128)} %bitcast.level, bf16[256,1920]{1,0:T(8,128)(2,1)S(1)} %copy-done.3, bf16[256,1920]{1,0:T(8,128)(2,1)} %collective-permute-done.4.got_ref, ...), custom_call_target="tpu_custom_call" | custom-call | flops 1024 | bytes 1024 | tf_op jit(solution)/shard_map/combine/pallas_call | solution.py:212
  78.8 1.8 %collective-permute-start.5 = (bf16[128,2048]{1,0:T(8,128)(2,1)}, bf16[128,2048]{1,0:T(8,128)(2,1)S(1)}, u32[]{:S(2)}, u32[]{:S(2)}) collective-permute-start(bf16[128,2048]{1,0:T(8,128)(2,1)} %get-tuple-element.43), channel_id=1, source_target_pairs={{0,16},{16,32},{32,48},{48,0},{1,17},{17,33},{33,49},{49,1},{2,18}... | collective-permute-start | bytes 1572872 | tf_op jit(solution)/shard_map/ppermute | solution.py:497
  80.6 2.7 %collective-permute-start.6 = (bf16[128,2048]{1,0:T(8,128)(2,1)}, bf16[128,2048]{1,0:T(8,128)(2,1)S(1)}, u32[]{:S(2)}, u32[]{:S(2)}) collective-permute-start(bf16[128,2048]{1,0:T(8,128)(2,1)} %get-tuple-element.44), channel_id=1, source_target_pairs={{0,32},{16,48},{32,0},{48,16},{1,33},{17,49},{33,1},{49,17},{2,34}... | collective-permute-start | bytes 1572872 | tf_op jit(solution)/shard_map/ppermute | solution.py:497
  83.3 1.4 collective-permute-start.7
  84.6 6.9 %collective-permute-done.2.refs_1_.got_ref = bf16[256,1920]{1,0:T(8,128)(2,1)} collective-permute-done((bf16[256,1920]{1,0:T(8,128)(2,1)}, bf16[256,1920]{1,0:T(8,128)(2,1)}, u32[]{:S(2)}, u32[]{:S(2)}) %collective-permute-start.2) | collective-permute-done | bytes 983072 | tf_op jit(solution)/shard_map/ppermute | solution.py:475
  91.8 1.3 copy-done.8
  93.1 4.4 %combine.4 = (bf16[256,5120]{1,0:T(8,128)(2,1)}, bf16[128,1920]{1,0:T(8,128)(2,1)S(1)}, bf16[128,1920]{1,0:T(8,128)(2,1)}, bf16[128,1920]{1,0:T(8,128)(2,1)S(1)}, bf16[128,1920]{1,0:T(8,128)(2,1)S(1)}) custom-call(f32[1]{0:T(128)} %bitcast.level, bf16[256,1920]{1,0:T(8,128)(2,1)S(1)} %copy-done.8, ...), custom_call_target="tpu_custom_call", output_to_operand_aliasing={{0}: (5, {})} | custom-call | flops 1024 | bytes 1024 | tf_op jit(solution)/shard_map/combine/pallas_call | solution.py:212
  97.5 0.8 copy-done.10
  99.1 1.2 collective-permute-start.11
  101.6 3.0 %collective-permute-start.12 = (bf16[128,1920]{1,0:T(8,128)(2,1)}, bf16[128,1920]{1,0:T(8,128)(2,1)}, u32[]{:S(2)}, u32[]{:S(2)}) collective-permute-start(bf16[128,1920]{1,0:T(8,128)(2,1)} %copy-done.15), channel_id=1, source_target_pairs={{0,32},{16,48},{32,0},{48,16},{1,33},{17,49},{33,1},{49,17},{2,34}... | collective-permute-start | bytes 1474568 | tf_op jit(solution)/shard_map/ppermute | solution.py:497
  104.6 1.1 collective-permute-start.13
  105.9 1.1 copy-done.9
  107.0 3.4 %combine.5 = (bf16[256,5120]{1,0:T(8,128)(2,1)}, bf16[128,1280]{1,0:T(8,128)(2,1)S(1)}, bf16[128,1280]{1,0:T(8,128)(2,1)}, bf16[128,1280]{1,0:T(8,128)(2,1)}, bf16[128,1280]{1,0:T(8,128)(2,1)}) custom-call(f32[1]{0:T(128)} %bitcast.level, bf16[256,1280]{1,0:T(8,128)(2,1)S(1)} %copy-done.9, ...), custom_call_target="tpu_custom_call", output_to_operand_aliasing={{0}: (5, {})} | custom-call | flops 1024 | bytes 1024 | tf_op jit(solution)/shard_map/combine/pallas_call | solution.py:212
  110.4 2.3 %collective-permute-start.10 = (bf16[128,1280]{1,0:T(8,128)(2,1)}, bf16[128,1280]{1,0:T(8,128)(2,1)}, u32[]{:S(2)}, u32[]{:S(2)}) collective-permute-start(bf16[128,1280]{1,0:T(8,128)(2,1)} %get-tuple-element.50), channel_id=1, source_target_pairs={{0,48},{16,0},{32,16},{48,32},{1,49},{17,1},{33,17},{49,33},{2,50}... | collective-permute-start | bytes 983048 | tf_op jit(solution)/shard_map/ppermute | solution.py:497
  113.8 9.3 %collective-permute-start.9 = (bf16[128,1280]{1,0:T(8,128)(2,1)}, bf16[128,1280]{1,0:T(8,128)(2,1)}, u32[]{:S(2)}, u32[]{:S(2)}) collective-permute-start(bf16[128,1280]{1,0:T(8,128)(2,1)} %get-tuple-element.49), channel_id=1, source_target_pairs={{0,32},{16,48},{32,0},{48,16},{1,33},{17,49},{33,1},{49,17},{2,34}... | collective-permute-start | bytes 983048 | tf_op jit(solution)/shard_map/ppermute | solution.py:497
  123.2 7.7 %teach.3 = (f32[544,1024]{1,0:T(8,128)}, f32[2,512,128]{2,1,0:T(8,128)S(1)}) custom-call(f32[4]{0:T(128)S(1)} %gather_fusion, bf16[128,2048]{1,0:T(8,128)(2,1)S(1)} %get-tuple-element.55.refs_1_.refs_10_, bf16[128,2048]{1,0:T(8,128)(2,1)S(1)} %collective-permute-done.5.refs_1_.refs_2_.refs_11_, ...), custom_call_target="tpu_custom_call" | custom-call | flops 1024 | bytes 1024 | tf_op jit(solution)/shard_map/teach/pallas_call | solution.py:362
  131.0 8.4 %teach.4 = (f32[544,1024]{1,0:T(8,128)}, f32[2,512,128]{2,1,0:T(8,128)S(1)}) custom-call(f32[4]{0:T(128)S(1)} %gather_fusion, bf16[128,1920]{1,0:T(8,128)(2,1)S(1)} %copy-done.11, bf16[128,1920]{1,0:T(8,128)(2,1)S(1)} %copy-done.13, bf16[128,1920]{1,0:T(8,128)(2,1)} %collective-permute-done.12.refs_3_, bf16[128,1920]{1,0:T(8,128)(2,1)} %collective-permute-done.13.refs_4_, ...), custom_call_target="tpu_custom_call" | custom-call | flops 1024 | bytes 1024 | tf_op jit(solution)/shard_map/teach/pallas_call | solution.py:362
  139.5 7.4 %teach.5 = (bf16[128,64]{1,0:T(8,128)(2,1)S(1)}, bf16[128,64]{1,0:T(8,128)(2,1)S(1)}, bf16[128,64]{1,0:T(8,128)(2,1)S(1)}, bf16[128,64]{1,0:T(8,128)(2,1)S(1)}) custom-call(f32[4]{0:T(128)S(1)} %gather_fusion, bf16[128,1280]{1,0:T(8,128)(2,1)S(1)} %copy-done.7, bf16[128,1280]{1,0:T(8,128)(2,1)} %collective-permute-done.8.refs_2_, ...), custom_call_target="tpu_custom_call" | custom-call | flops 1024 | bytes 1024 | tf_op jit(solution)/shard_map/teach/pallas_call | solution.py:362
  146.9 1.3 collective-permute-start.14
  148.2 1.2 collective-permute-start.15
  149.7 2.7 %collective-permute-done.15.refs_2_ = bf16[128,64]{1,0:T(8,128)(2,1)S(1)} collective-permute-done((bf16[128,64]{1,0:T(8,128)(2,1)S(1)}, bf16[128,64]{1,0:T(8,128)(2,1)S(1)}, u32[]{:S(2)}, u32[]{:S(2)}) %collective-permute-start.15) | collective-permute-done | bytes 16416 | tf_op jit(solution)/shard_map/ppermute | solution.py:525
  152.5 0.8 collective-permute-done.16.refs_3_
  (81 shorter events, 7.7 us)
Async XLA Ops:
  7.2 61.4 %copy-start = (f32[32,2,5120]{2,1,0:T(2,128)S(1)}, f32[32,2,5120]{2,1,0:T(2,128)}, u32[]{:S(2)}) copy-start(f32[32,2,5120]{2,1,0:T(2,128)} %param.19) | copy-start | bytes 3932164
  7.2 41.8 %all-gather.3.cloned.1.call-start = ((), (), s32[]{:S(2)}) async-start(), calls=%async_computation | async-start | bytes 1679360 | tf_op jit(solution)/shard_map/all_gather | solution.py:444
  7.2 17.3 %collective-permute-start = (bf16[512,2560]{1,0:T(8,128)(2,1)}, bf16[512,2560]{1,0:T(8,128)(2,1)}, u32[]{:S(2)}, u32[]{:S(2)}) collective-permute-start(bf16[512,2560]{1,0:T(8,128)(2,1)} %bitcast.39), channel_id=1, source_target_pairs={{0,64},{1,65},{2,66},{3,67},{4,68},{5,69},{6,70},{7,71},{8,72},{9,... | collective-permute-start | bytes 7864328 | tf_op jit(solution)/shard_map/ppermute | solution.py:434
  8.7 15.9 %collective-permute-start.1 = (bf16[512,2560]{1,0:T(8,128)(2,1)}, bf16[512,2560]{1,0:T(8,128)(2,1)}, u32[]{:S(2)}, u32[]{:S(2)}) collective-permute-start(bf16[512,2560]{1,0:T(8,128)(2,1)} %bitcast.41), channel_id=1, source_target_pairs={{0,64},{1,65},{2,66},{3,67},{4,68},{5,69},{6,70},{7,71},{8,72},{9,... | collective-permute-start | bytes 7864328 | tf_op jit(solution)/shard_map/ppermute | solution.py:435
  13.2 109.9 %all-gather.5.cloned.1.call-start = ((), (), s32[]{:S(2)}) async-start(), calls=%async_computation.1 | async-start | bytes 12091392 | tf_op jit(solution)/shard_map/all_gather | solution.py:472
  49.1 18.2 %copy-start.18 = (s32[1,1,256,1]{2,3,1,0:T(1,128)S(1)}, s32[1,1,256,1]{2,3,1,0:T(1,128)}, u32[]{:S(2)}) copy-start(s32[1,1,256,1]{2,3,1,0:T(1,128)} %param.17) | copy-start | bytes 3076
  49.1 24.8 %copy-start.3 = (bf16[256,1920]{1,0:T(8,128)(2,1)S(1)}, bf16[256,1920]{1,0:T(8,128)(2,1)}, u32[]{:S(2)}) copy-start(bf16[256,1920]{1,0:T(8,128)(2,1)} %get-tuple-element.40.kept_ref.refs_1_) | copy-start | bytes 2949124
  49.1 24.8 %collective-permute-start.4 = (bf16[256,1920]{1,0:T(8,128)(2,1)}, bf16[256,1920]{1,0:T(8,128)(2,1)}, u32[]{:S(2)}, u32[]{:S(2)}) collective-permute-start(bf16[256,1920]{1,0:T(8,128)(2,1)} %get-tuple-element.35.refs_0_), channel_id=1, source_target_pairs={{0,1},{1,0},{2,3},{3,2},{4,5},{5,4},{6,7},{7,6},{8,9},{9,8},{10,11... | collective-permute-start | bytes 2949128 | tf_op jit(solution)/shard_map/ppermute | solution.py:475
  67.2 24.3 %collective-permute-start.2 = (bf16[256,1920]{1,0:T(8,128)(2,1)}, bf16[256,1920]{1,0:T(8,128)(2,1)}, u32[]{:S(2)}, u32[]{:S(2)}) collective-permute-start(bf16[256,1920]{1,0:T(8,128)(2,1)} %get-tuple-element.38), channel_id=1, source_target_pairs={{0,1},{1,0},{2,3},{3,2},{4,5},{5,4},{6,7},{7,6},{8,9},{9,8},{10,11... | collective-permute-start | bytes 2949128 | tf_op jit(solution)/shard_map/ppermute | solution.py:475
  78.8 44.4 %copy-start.4 = (bf16[128,2048]{1,0:T(8,128)(2,1)}, bf16[128,2048]{1,0:T(8,128)(2,1)S(1)}, u32[]{:S(2)}) copy-start(bf16[128,2048]{1,0:T(8,128)(2,1)S(1)} %get-tuple-element.55.refs_1_.refs_10_) | copy-start | bytes 1572868
  78.8 22.8 %collective-permute-start.5 = (bf16[128,2048]{1,0:T(8,128)(2,1)}, bf16[128,2048]{1,0:T(8,128)(2,1)S(1)}, u32[]{:S(2)}, u32[]{:S(2)}) collective-permute-start(bf16[128,2048]{1,0:T(8,128)(2,1)} %get-tuple-element.43), channel_id=1, source_target_pairs={{0,16},{16,32},{32,48},{48,0},{1,17},{17,33},{33,49},{49,1},{2,18}... | collective-permute-start | bytes 1572872 | tf_op jit(solution)/shard_map/ppermute | solution.py:497
  80.6 24.0 %collective-permute-start.6 = (bf16[128,2048]{1,0:T(8,128)(2,1)}, bf16[128,2048]{1,0:T(8,128)(2,1)S(1)}, u32[]{:S(2)}, u32[]{:S(2)}) collective-permute-start(bf16[128,2048]{1,0:T(8,128)(2,1)} %get-tuple-element.44), channel_id=1, source_target_pairs={{0,32},{16,48},{32,0},{48,16},{1,33},{17,49},{33,1},{49,17},{2,34}... | collective-permute-start | bytes 1572872 | tf_op jit(solution)/shard_map/ppermute | solution.py:497
  83.3 22.4 %collective-permute-start.7 = (bf16[128,2048]{1,0:T(8,128)(2,1)}, bf16[128,2048]{1,0:T(8,128)(2,1)S(1)}, u32[]{:S(2)}, u32[]{:S(2)}) collective-permute-start(bf16[128,2048]{1,0:T(8,128)(2,1)} %get-tuple-element.45), channel_id=1, source_target_pairs={{0,48},{16,0},{32,16},{48,32},{1,49},{17,1},{33,17},{49,33},{2,50}... | collective-permute-start | bytes 1572872 | tf_op jit(solution)/shard_map/ppermute | solution.py:497
  91.5 14.4 %collective-permute-start.3 = (bf16[256,1280]{1,0:T(8,128)(2,1)}, bf16[256,1280]{1,0:T(8,128)(2,1)}, u32[]{:S(2)}, u32[]{:S(2)}) collective-permute-start(bf16[256,1280]{1,0:T(8,128)(2,1)} %after.2), channel_id=1, source_target_pairs={{0,1},{1,0},{2,3},{3,2},{4,5},{5,4},{6,7},{7,6},{8,9},{9,8},{10,11... | collective-permute-start | bytes 1966088 | tf_op jit(solution)/shard_map/ppermute | solution.py:476
  93.1 7.9 %copy-start.16 = (f32[32]{0:T(128)S(1)}, f32[32]{0:T(128)}, u32[]{:S(2)}) copy-start(f32[32]{0:T(128)} %param.20) | copy-start | bytes 388
  99.1 13.9 %collective-permute-start.11 = (bf16[128,1920]{1,0:T(8,128)(2,1)}, bf16[128,1920]{1,0:T(8,128)(2,1)S(1)}, u32[]{:S(2)}, u32[]{:S(2)}) collective-permute-start(bf16[128,1920]{1,0:T(8,128)(2,1)} %get-tuple-element.52), channel_id=1, source_target_pairs={{0,16},{16,32},{32,48},{48,0},{1,17},{17,33},{33,49},{49,1},{2,18}... | collective-permute-start | bytes 1474568 | tf_op jit(solution)/shard_map/ppermute | solution.py:497
  101.6 29.3 %collective-permute-start.12 = (bf16[128,1920]{1,0:T(8,128)(2,1)}, bf16[128,1920]{1,0:T(8,128)(2,1)}, u32[]{:S(2)}, u32[]{:S(2)}) collective-permute-start(bf16[128,1920]{1,0:T(8,128)(2,1)} %copy-done.15), channel_id=1, source_target_pairs={{0,32},{16,48},{32,0},{48,16},{1,33},{17,49},{33,1},{49,17},{2,34}... | collective-permute-start | bytes 1474568 | tf_op jit(solution)/shard_map/ppermute | solution.py:497
  104.6 26.4 %collective-permute-start.13 = (bf16[128,1920]{1,0:T(8,128)(2,1)}, bf16[128,1920]{1,0:T(8,128)(2,1)}, u32[]{:S(2)}, u32[]{:S(2)}) collective-permute-start(bf16[128,1920]{1,0:T(8,128)(2,1)} %copy-done.14), channel_id=1, source_target_pairs={{0,48},{16,0},{32,16},{48,32},{1,49},{17,1},{33,17},{49,33},{2,50}... | collective-permute-start | bytes 1474568 | tf_op jit(solution)/shard_map/ppermute | solution.py:497
  105.6 17.5 %copy-start.2 = (bf16[128,2048]{1,0:T(8,128)(2,1)}, bf16[128,2048]{1,0:T(8,128)(2,1)S(1)}, u32[]{:S(2)}) copy-start(bf16[128,2048]{1,0:T(8,128)(2,1)S(1)} %collective-permute-done.7.refs_3_.refs_4_.refs_13_) | copy-start | bytes 1572868
  107.0 16.1 %copy-start.17 = (bf16[8,5120]{1,0:T(8,128)(2,1)S(1)}, bf16[8,5120]{1,0:T(8,128)(2,1)}, u32[]{:S(2)}) copy-start(bf16[8,5120]{1,0:T(8,128)(2,1)} %get-tuple-element.76) | copy-start | bytes 245764
  110.4 20.6 %copy-start.6 = (bf16[128,1280]{1,0:T(8,128)(2,1)}, bf16[128,1280]{1,0:T(8,128)(2,1)S(1)}, u32[]{:S(2)}) copy-start(bf16[128,1280]{1,0:T(8,128)(2,1)S(1)} %get-tuple-element.47.refs_8_.refs_1_) | copy-start | bytes 983044
  110.4 29.1 %collective-permute-start.10 = (bf16[128,1280]{1,0:T(8,128)(2,1)}, bf16[128,1280]{1,0:T(8,128)(2,1)}, u32[]{:S(2)}, u32[]{:S(2)}) collective-permute-start(bf16[128,1280]{1,0:T(8,128)(2,1)} %get-tuple-element.50), channel_id=1, source_target_pairs={{0,48},{16,0},{32,16},{48,32},{1,49},{17,1},{33,17},{49,33},{2,50}... | collective-permute-start | bytes 983048 | tf_op jit(solution)/shard_map/ppermute | solution.py:497
  112.7 26.7 %collective-permute-start.8 = (bf16[128,1280]{1,0:T(8,128)(2,1)}, bf16[128,1280]{1,0:T(8,128)(2,1)}, u32[]{:S(2)}, u32[]{:S(2)}) collective-permute-start(bf16[128,1280]{1,0:T(8,128)(2,1)} %get-tuple-element.48), channel_id=1, source_target_pairs={{0,16},{16,32},{32,48},{48,0},{1,17},{17,33},{33,49},{49,1},{2,18}... | collective-permute-start | bytes 983048 | tf_op jit(solution)/shard_map/ppermute | solution.py:497
  113.8 25.7 %collective-permute-start.9 = (bf16[128,1280]{1,0:T(8,128)(2,1)}, bf16[128,1280]{1,0:T(8,128)(2,1)}, u32[]{:S(2)}, u32[]{:S(2)}) collective-permute-start(bf16[128,1280]{1,0:T(8,128)(2,1)} %get-tuple-element.49), channel_id=1, source_target_pairs={{0,32},{16,48},{32,0},{48,16},{1,33},{17,49},{33,1},{49,17},{2,34}... | collective-permute-start | bytes 983048 | tf_op jit(solution)/shard_map/ppermute | solution.py:497
  123.2 7.8 %copy-start.11 = (bf16[128,1920]{1,0:T(8,128)(2,1)S(1)}, bf16[128,1920]{1,0:T(8,128)(2,1)}, u32[]{:S(2)}) copy-start(bf16[128,1920]{1,0:T(8,128)(2,1)} %copy-done.10) | copy-start | bytes 1474564
  123.2 7.8 %copy-start.13 = (bf16[128,1920]{1,0:T(8,128)(2,1)S(1)}, bf16[128,1920]{1,0:T(8,128)(2,1)}, u32[]{:S(2)}) copy-start(bf16[128,1920]{1,0:T(8,128)(2,1)} %copy-done.12) | copy-start | bytes 1474564
  131.0 8.5 %copy-start.5 = (bf16[128,2048]{1,0:T(8,128)(2,1)S(1)}, bf16[128,2048]{1,0:T(8,128)(2,1)}, u32[]{:S(2)}) copy-start(bf16[128,2048]{1,0:T(8,128)(2,1)} %copy-done.4) | copy-start | bytes 1572868
  131.0 8.5 %copy-start.7 = (bf16[128,1280]{1,0:T(8,128)(2,1)S(1)}, bf16[128,1280]{1,0:T(8,128)(2,1)}, u32[]{:S(2)}) copy-start(bf16[128,1280]{1,0:T(8,128)(2,1)} %copy-done.6) | copy-start | bytes 983044
  139.5 14.8 %copy-start.1 = (f32[32,2,5120]{2,1,0:T(2,128)S(1)}, f32[32,2,5120]{2,1,0:T(2,128)}, u32[]{:S(2)}) copy-start(f32[32,2,5120]{2,1,0:T(2,128)} %param.19) | copy-start | bytes 3932164
  146.9 2.8 %collective-permute-start.14 = (bf16[128,64]{1,0:T(8,128)(2,1)S(1)}, bf16[128,64]{1,0:T(8,128)(2,1)S(1)}, u32[]{:S(2)}, u32[]{:S(2)}) collective-permute-start(bf16[128,64]{1,0:T(8,128)(2,1)S(1)} %get-tuple-element.61), channel_id=1, source_target_pairs={{0,48},{16,0},{32,16},{48,32},{1,49},{17,1},{33,17},{49,33},{2,50}... | collective-permute-start | bytes 49160 | tf_op jit(solution)/shard_map/ppermute | solution.py:525
  148.2 4.3 %collective-permute-start.15 = (bf16[128,64]{1,0:T(8,128)(2,1)S(1)}, bf16[128,64]{1,0:T(8,128)(2,1)S(1)}, u32[]{:S(2)}, u32[]{:S(2)}) collective-permute-start(bf16[128,64]{1,0:T(8,128)(2,1)S(1)} %get-tuple-element.62), channel_id=1, source_target_pairs={{0,32},{16,48},{32,0},{48,16},{1,33},{17,49},{33,1},{49,17},{2,34}... | collective-permute-start | bytes 49160 | tf_op jit(solution)/shard_map/ppermute | solution.py:525
  149.3 4.0 %collective-permute-start.16 = (bf16[128,64]{1,0:T(8,128)(2,1)S(1)}, bf16[128,64]{1,0:T(8,128)(2,1)S(1)}, u32[]{:S(2)}, u32[]{:S(2)}) collective-permute-start(bf16[128,64]{1,0:T(8,128)(2,1)S(1)} %get-tuple-element.63), channel_id=1, source_target_pairs={{0,16},{16,32},{32,48},{48,0},{1,17},{17,33},{33,49},{49,1},{2,18}... | collective-permute-start | bytes 49160 | tf_op jit(solution)/shard_map/ppermute | solution.py:525
  (6 other events, 6.0 us)
Sparse Core Ops, SparseCore 0:
  13.3 30.8 all-gather.2
  49.2 62.7 all-gather.4

commit v3 on v2

--- a/solution.py
+++ b/solution.py
@@ -100,8 +100,8 @@
             acc = dot_nn(weights.astype(BF16), v_ref[:, cols])
             gap = stat_ref[:, cols] - (peak * SCALE2 + jnp.log2(total))
             share_own = 1.0 / (1.0 + jnp.exp2(-gap))
-            share_early = 1.0 / (1.0 + jnp.exp2(gap))
-            merged = share_own * own_ref[:, cols].astype(F32) + (share_early / total) * acc
+            early = acc / total
+            merged = early + share_own * (own_ref[:, cols].astype(F32) - early)
             o_ref[:, cols] = merged.astype(BF16)
 
 

time: 162 us -> 162 us (level)
  waiting for transfers between devices: 15.7 us -> 22.6 us
  starting transfers between devices: 30.5 us -> 24.7 us
    ppermute x9, starting transfers between devices: 22.8 us -> 14.3 us  [send(): lax.ppermute(blocks[d], 'z', along(z_count, d))]
    ppermute x9, waiting for transfers between devices: 0.28 us -> 5.06 us  [send(): lax.ppermute(blocks[d], 'z', along(z_count, d))]
    ppermute x3, starting transfers between devices: 2.46 us -> 5.15 us  [shards(): lax.ppermute(carry[d], 'z', along(z_count, z_count - d))]
  transfers between devices with their start and end apart: 19 -> 19, of which waited for: 7 -> 9; matrix products, arithmetic and copies ran while one was open for 4% -> 4% of each run, Pallas kernels for 50% -> 49%
where the time goes in v3:
time: 162 us; the launch traced here: 161 us
  Pallas kernels  87.3 us (54%)
  starting transfers between devices  24.7 us (15%)
  waiting for transfers between devices  22.6 us (14%)
  between operations  15 us (9%)
  local copies, waits for them, and re-layouts  7.21 us (4%)
  other arithmetic  4.4 us (3%)
    pallas_call x2, Pallas kernels, project(): pl.pallas_call(functools.partial(project_kernel, counts), grid_spec=pltpu...  26.9 us
    pallas_call x3, Pallas kernels, teach(): pl.pallas_call(functools.partial(teach_kernel, groups, feats, width, carr...  23.6 us
    ppermute x9, starting transfers between devices, send(): lax.ppermute(blocks[d], 'z', along(z_count, d))  14.3 us
    pallas_call x1, Pallas kernels, attend_early(): pl.pallas_call(attend_early_kernel, grid_spec=pltpu.PrefetchScalarGridSpe...  12.7 us
    pallas_call x3, Pallas kernels, combine(): pl.pallas_call(functools.partial(combine_kernel, groups, steps, tags is n...  12.7 us
    pallas_call x1, Pallas kernels, attend_own(): pl.pallas_call(attend_own_kernel, grid=(width // wide,), in_specs=[block]...  11.3 us
    ppermute x1, waiting for transfers between devices, shards(): lax.ppermute(sent[1], 'xl', swap)  7.78 us
    unnamed x39, local copies, waits for them, and re-layouts  5.45 us
  transfers between devices with their start and end apart: 19, of which 9 were waited for; matrix products, arithmetic and copies ran while one was open for 4% of the time, Pallas kernels for 49%

profile of v3, /device:TPU:1, one launch (start us, length us, event | category | flops | bytes accessed | tf_op | source)
XLA Modules:
  0.0 161.2 jit_solution(3322550614438744243)
XLA Ops:
  7.2 1.4 collective-permute-start
  8.7 1.3 collective-permute-start.1
  10.0 0.9 fusion.21
  10.9 1.4 fusion.1
  13.3 11.3 %attend_own.1 = (bf16[512,2560]{1,0:T(8,128)(2,1)}, f32[512,2560]{1,0:T(8,128)}) custom-call(bf16[512,2560]{1,0:T(8,128)(2,1)} %bitcast.43, bf16[512,2560]{1,0:T(8,128)(2,1)} %bitcast.40, bf16[512,2560]{1,0:T(8,128)(2,1)} %bitcast.42), custom_call_target="tpu_custom_call" | custom-call | flops 5368709120 | bytes 10485760 | tf_op jit(solution)/shard_map/attend_own/pallas_call | solution.py:72
  24.5 12.7 %attend_early.1.a_ref = bf16[512,2560]{1,0:T(8,128)(2,1)} custom-call(s32[1]{0:T(128)} %bitcast.2.info, bf16[512,2560]{1,0:T(8,128)(2,1)} %bitcast.44, bf16[512,2560]{1,0:T(8,128)(2,1)} %collective-permute-done.k_ref, bf16[512,2560]{1,0:T(8,128)(2,1)} %collective-permute-done.1.v_ref, ...), custom_call_target="tpu_custom_call", output_to_operand_aliasing={{}: (4, {})} | custom-call | flops 5368709120 | bytes 13107200 | tf_op jit(solution)/shard_map/attend_early/pallas_call | solution.py:112
  37.2 10.9 %project.2 = (bf16[256,1920]{1,0:T(8,128)(2,1)}, bf16[256,1920]{1,0:T(8,128)(2,1)}) custom-call(s32[1]{0:T(128)} %bitcast.1.info, bf16[512,2560]{1,0:T(8,128)(2,1)} %attend_early.1.a_ref, bf16[2560,5120]{1,0:T(8,128)(2,1)} %w_ref.3), custom_call_target="tpu_custom_call" | custom-call | flops 5033164800 | bytes 9830400 | tf_op jit(solution)/shard_map/project/pallas_call | solution.py:155
  48.2 2.1 %collective-permute-start.4 = (bf16[256,1920]{1,0:T(8,128)(2,1)}, bf16[256,1920]{1,0:T(8,128)(2,1)}, u32[]{:S(2)}, u32[]{:S(2)}) collective-permute-start(bf16[256,1920]{1,0:T(8,128)(2,1)} %get-tuple-element.35.refs_0_), channel_id=1, source_target_pairs={{0,1},{1,0},{2,3},{3,2},{4,5},{5,4},{6,7},{7,6},{8,9},{9,8},{10,11... | collective-permute-start | bytes 2949128 | tf_op jit(solution)/shard_map/ppermute | solution.py:475
  50.3 16.0 %project.3 = (bf16[256,1920]{1,0:T(8,128)(2,1)}, bf16[256,1280]{1,0:T(8,128)(2,1)}, bf16[256,1920]{1,0:T(8,128)(2,1)}, bf16[256,1280]{1,0:T(8,128)(2,1)}) custom-call(s32[1]{0:T(128)} %bitcast.1.info, bf16[512,2560]{1,0:T(8,128)(2,1)} %attend_early.1.a_ref, bf16[2560,5120]{1,0:T(8,128)(2,1)} %w_ref.3, bf16[256,1920]{1,0:T(8,128)(2,1)} %get-tuple-element.35.refs_0_), custom_call_target="tpu_custom_call" | custom-call | flops 8388608000 | bytes 16384000 | tf_op jit(solution)/shard_map/project/pallas_call | solution.py:155
  68.6 4.4 %collective-permute-done.4.got_ref = bf16[256,1920]{1,0:T(8,128)(2,1)} collective-permute-done((bf16[256,1920]{1,0:T(8,128)(2,1)}, bf16[256,1920]{1,0:T(8,128)(2,1)}, u32[]{:S(2)}, u32[]{:S(2)}) %collective-permute-start.4) | collective-permute-done | bytes 983072 | tf_op jit(solution)/shard_map/ppermute | solution.py:475
  73.0 4.8 %combine.3 = (bf16[256,5120]{1,0:T(8,128)(2,1)}, bf16[128,2048]{1,0:T(8,128)(2,1)S(1)}, bf16[128,2048]{1,0:T(8,128)(2,1)}, bf16[128,2048]{1,0:T(8,128)(2,1)}, bf16[128,2048]{1,0:T(8,128)(2,1)}) custom-call(f32[1]{0:T(128)} %bitcast.level, bf16[256,1920]{1,0:T(8,128)(2,1)S(1)} %copy-done.3, bf16[256,1920]{1,0:T(8,128)(2,1)} %collective-permute-done.4.got_ref, ...), custom_call_target="tpu_custom_call" | custom-call | flops 1024 | bytes 1024 | tf_op jit(solution)/shard_map/combine/pallas_call | solution.py:212
  77.9 1.8 %collective-permute-start.5 = (bf16[128,2048]{1,0:T(8,128)(2,1)}, bf16[128,2048]{1,0:T(8,128)(2,1)S(1)}, u32[]{:S(2)}, u32[]{:S(2)}) collective-permute-start(bf16[128,2048]{1,0:T(8,128)(2,1)} %get-tuple-element.43), channel_id=1, source_target_pairs={{0,16},{16,32},{32,48},{48,0},{1,17},{17,33},{33,49},{49,1},{2,18}... | collective-permute-start | bytes 1572872 | tf_op jit(solution)/shard_map/ppermute | solution.py:497
  79.7 3.3 %collective-permute-start.6 = (bf16[128,2048]{1,0:T(8,128)(2,1)}, bf16[128,2048]{1,0:T(8,128)(2,1)S(1)}, u32[]{:S(2)}, u32[]{:S(2)}) collective-permute-start(bf16[128,2048]{1,0:T(8,128)(2,1)} %get-tuple-element.44), channel_id=1, source_target_pairs={{0,32},{16,48},{32,0},{48,16},{1,33},{17,49},{33,1},{49,17},{2,34}... | collective-permute-start | bytes 1572872 | tf_op jit(solution)/shard_map/ppermute | solution.py:497
  83.7 7.8 %collective-permute-done.2.refs_1_.got_ref = bf16[256,1920]{1,0:T(8,128)(2,1)} collective-permute-done((bf16[256,1920]{1,0:T(8,128)(2,1)}, bf16[256,1920]{1,0:T(8,128)(2,1)}, u32[]{:S(2)}, u32[]{:S(2)}) %collective-permute-start.2) | collective-permute-done | bytes 983072 | tf_op jit(solution)/shard_map/ppermute | solution.py:475
  91.8 1.2 copy-done.8
  93.0 4.4 %combine.4 = (bf16[256,5120]{1,0:T(8,128)(2,1)}, bf16[128,1920]{1,0:T(8,128)(2,1)S(1)}, bf16[128,1920]{1,0:T(8,128)(2,1)}, bf16[128,1920]{1,0:T(8,128)(2,1)S(1)}, bf16[128,1920]{1,0:T(8,128)(2,1)S(1)}) custom-call(f32[1]{0:T(128)} %bitcast.level, bf16[256,1920]{1,0:T(8,128)(2,1)S(1)} %copy-done.8, ...), custom_call_target="tpu_custom_call", output_to_operand_aliasing={{0}: (5, {})} | custom-call | flops 1024 | bytes 1024 | tf_op jit(solution)/shard_map/combine/pallas_call | solution.py:212
  99.0 1.3 collective-permute-start.11
  101.6 2.8 %collective-permute-start.12 = (bf16[128,1920]{1,0:T(8,128)(2,1)}, bf16[128,1920]{1,0:T(8,128)(2,1)}, u32[]{:S(2)}, u32[]{:S(2)}) collective-permute-start(bf16[128,1920]{1,0:T(8,128)(2,1)} %copy-done.15), channel_id=1, source_target_pairs={{0,32},{16,48},{32,0},{48,16},{1,33},{17,49},{33,1},{49,17},{2,34}... | collective-permute-start | bytes 1474568 | tf_op jit(solution)/shard_map/ppermute | solution.py:497
  105.4 1.5 collective-permute-done.3.got_ref
  106.8 1.1 copy-done.9
  107.9 3.4 %combine.5 = (bf16[256,5120]{1,0:T(8,128)(2,1)}, bf16[128,1280]{1,0:T(8,128)(2,1)S(1)}, bf16[128,1280]{1,0:T(8,128)(2,1)}, bf16[128,1280]{1,0:T(8,128)(2,1)}, bf16[128,1280]{1,0:T(8,128)(2,1)}) custom-call(f32[1]{0:T(128)} %bitcast.level, bf16[256,1280]{1,0:T(8,128)(2,1)S(1)} %copy-done.9, ...), custom_call_target="tpu_custom_call", output_to_operand_aliasing={{0}: (5, {})} | custom-call | flops 1024 | bytes 1024 | tf_op jit(solution)/shard_map/combine/pallas_call | solution.py:212
  111.3 1.5 collective-permute-start.10
  114.4 1.9 %collective-permute-start.9 = (bf16[128,1280]{1,0:T(8,128)(2,1)}, bf16[128,1280]{1,0:T(8,128)(2,1)}, u32[]{:S(2)}, u32[]{:S(2)}) collective-permute-start(bf16[128,1280]{1,0:T(8,128)(2,1)} %get-tuple-element.49), channel_id=1, source_target_pairs={{0,32},{16,48},{32,0},{48,16},{1,33},{17,49},{33,1},{49,17},{2,34}... | collective-permute-start | bytes 983048 | tf_op jit(solution)/shard_map/ppermute | solution.py:497
  116.4 7.7 %teach.3 = (f32[544,1024]{1,0:T(8,128)}, f32[2,512,128]{2,1,0:T(8,128)S(1)}) custom-call(f32[4]{0:T(128)S(1)} %gather_fusion, bf16[128,2048]{1,0:T(8,128)(2,1)S(1)} %get-tuple-element.55.refs_1_.refs_10_, bf16[128,2048]{1,0:T(8,128)(2,1)S(1)} %collective-permute-done.5.refs_1_.refs_2_.refs_11_, ...), custom_call_target="tpu_custom_call" | custom-call | flops 1024 | bytes 1024 | tf_op jit(solution)/shard_map/teach/pallas_call | solution.py:362
  124.2 1.4 collective-permute-done.12.refs_3_
  125.5 1.8 %collective-permute-done.13.refs_4_ = bf16[128,1920]{1,0:T(8,128)(2,1)} collective-permute-done((bf16[128,1920]{1,0:T(8,128)(2,1)}, bf16[128,1920]{1,0:T(8,128)(2,1)}, u32[]{:S(2)}, u32[]{:S(2)}) %collective-permute-start.13) | collective-permute-done | bytes 491552 | tf_op jit(solution)/shard_map/ppermute | solution.py:497
  127.4 8.4 %teach.4 = (f32[544,1024]{1,0:T(8,128)}, f32[2,512,128]{2,1,0:T(8,128)S(1)}) custom-call(f32[4]{0:T(128)S(1)} %gather_fusion, bf16[128,1920]{1,0:T(8,128)(2,1)S(1)} %copy-done.11, bf16[128,1920]{1,0:T(8,128)(2,1)S(1)} %copy-done.13, bf16[128,1920]{1,0:T(8,128)(2,1)} %collective-permute-done.12.refs_3_, bf16[128,1920]{1,0:T(8,128)(2,1)} %collective-permute-done.13.refs_4_, ...), custom_call_target="tpu_custom_call" | custom-call | flops 1024 | bytes 1024 | tf_op jit(solution)/shard_map/teach/pallas_call | solution.py:362
  135.8 1.1 collective-permute-done.9.refs_3_
  136.9 7.4 %teach.5 = (bf16[128,64]{1,0:T(8,128)(2,1)S(1)}, bf16[128,64]{1,0:T(8,128)(2,1)S(1)}, bf16[128,64]{1,0:T(8,128)(2,1)S(1)}, bf16[128,64]{1,0:T(8,128)(2,1)S(1)}) custom-call(f32[4]{0:T(128)S(1)} %gather_fusion, bf16[128,1280]{1,0:T(8,128)(2,1)S(1)} %copy-done.7, bf16[128,1280]{1,0:T(8,128)(2,1)} %collective-permute-done.8.refs_2_, ...), custom_call_target="tpu_custom_call" | custom-call | flops 1024 | bytes 1024 | tf_op jit(solution)/shard_map/teach/pallas_call | solution.py:362
  144.3 4.0 %collective-permute-start.14 = (bf16[128,64]{1,0:T(8,128)(2,1)S(1)}, bf16[128,64]{1,0:T(8,128)(2,1)S(1)}, u32[]{:S(2)}, u32[]{:S(2)}) collective-permute-start(bf16[128,64]{1,0:T(8,128)(2,1)S(1)} %get-tuple-element.61), channel_id=1, source_target_pairs={{0,48},{16,0},{32,16},{48,32},{1,49},{17,1},{33,17},{49,33},{2,50}... | collective-permute-start | bytes 49160 | tf_op jit(solution)/shard_map/ppermute | solution.py:525
  148.3 1.2 collective-permute-start.15
  149.6 3.0 %collective-permute-done.15.refs_2_ = bf16[128,64]{1,0:T(8,128)(2,1)S(1)} collective-permute-done((bf16[128,64]{1,0:T(8,128)(2,1)S(1)}, bf16[128,64]{1,0:T(8,128)(2,1)S(1)}, u32[]{:S(2)}, u32[]{:S(2)}) %collective-permute-start.15) | collective-permute-done | bytes 16416 | tf_op jit(solution)/shard_map/ppermute | solution.py:525
  (81 shorter events, 11.0 us)
Async XLA Ops:
  7.2 60.5 %copy-start = (f32[32,2,5120]{2,1,0:T(2,128)S(1)}, f32[32,2,5120]{2,1,0:T(2,128)}, u32[]{:S(2)}) copy-start(f32[32,2,5120]{2,1,0:T(2,128)} %param.19) | copy-start | bytes 3932164
  7.2 40.9 %all-gather.3.cloned.1.call-start = ((), (), s32[]{:S(2)}) async-start(), calls=%async_computation | async-start | bytes 1679360 | tf_op jit(solution)/shard_map/all_gather | solution.py:444
  7.2 17.3 %collective-permute-start = (bf16[512,2560]{1,0:T(8,128)(2,1)}, bf16[512,2560]{1,0:T(8,128)(2,1)}, u32[]{:S(2)}, u32[]{:S(2)}) collective-permute-start(bf16[512,2560]{1,0:T(8,128)(2,1)} %bitcast.39), channel_id=1, source_target_pairs={{0,64},{1,65},{2,66},{3,67},{4,68},{5,69},{6,70},{7,71},{8,72},{9,... | collective-permute-start | bytes 7864328 | tf_op jit(solution)/shard_map/ppermute | solution.py:434
  8.7 15.9 %collective-permute-start.1 = (bf16[512,2560]{1,0:T(8,128)(2,1)}, bf16[512,2560]{1,0:T(8,128)(2,1)}, u32[]{:S(2)}, u32[]{:S(2)}) collective-permute-start(bf16[512,2560]{1,0:T(8,128)(2,1)} %bitcast.41), channel_id=1, source_target_pairs={{0,64},{1,65},{2,66},{3,67},{4,68},{5,69},{6,70},{7,71},{8,72},{9,... | collective-permute-start | bytes 7864328 | tf_op jit(solution)/shard_map/ppermute | solution.py:435
  13.2 103.2 %all-gather.5.cloned.1.call-start = ((), (), s32[]{:S(2)}) async-start(), calls=%async_computation.1 | async-start | bytes 12091392 | tf_op jit(solution)/shard_map/all_gather | solution.py:472
  48.2 18.2 %copy-start.18 = (s32[1,1,256,1]{2,3,1,0:T(1,128)S(1)}, s32[1,1,256,1]{2,3,1,0:T(1,128)}, u32[]{:S(2)}) copy-start(s32[1,1,256,1]{2,3,1,0:T(1,128)} %param.17) | copy-start | bytes 3076
  48.2 24.8 %copy-start.3 = (bf16[256,1920]{1,0:T(8,128)(2,1)S(1)}, bf16[256,1920]{1,0:T(8,128)(2,1)}, u32[]{:S(2)}) copy-start(bf16[256,1920]{1,0:T(8,128)(2,1)} %get-tuple-element.40.kept_ref.refs_1_) | copy-start | bytes 2949124
  48.2 24.8 %collective-permute-start.4 = (bf16[256,1920]{1,0:T(8,128)(2,1)}, bf16[256,1920]{1,0:T(8,128)(2,1)}, u32[]{:S(2)}, u32[]{:S(2)}) collective-permute-start(bf16[256,1920]{1,0:T(8,128)(2,1)} %get-tuple-element.35.refs_0_), channel_id=1, source_target_pairs={{0,1},{1,0},{2,3},{3,2},{4,5},{5,4},{6,7},{7,6},{8,9},{9,8},{10,11... | collective-permute-start | bytes 2949128 | tf_op jit(solution)/shard_map/ppermute | solution.py:475
  66.3 25.2 %collective-permute-start.2 = (bf16[256,1920]{1,0:T(8,128)(2,1)}, bf16[256,1920]{1,0:T(8,128)(2,1)}, u32[]{:S(2)}, u32[]{:S(2)}) collective-permute-start(bf16[256,1920]{1,0:T(8,128)(2,1)} %get-tuple-element.38), channel_id=1, source_target_pairs={{0,1},{1,0},{2,3},{3,2},{4,5},{5,4},{6,7},{7,6},{8,9},{9,8},{10,11... | collective-permute-start | bytes 2949128 | tf_op jit(solution)/shard_map/ppermute | solution.py:475
  77.9 38.5 %copy-start.4 = (bf16[128,2048]{1,0:T(8,128)(2,1)}, bf16[128,2048]{1,0:T(8,128)(2,1)S(1)}, u32[]{:S(2)}) copy-start(bf16[128,2048]{1,0:T(8,128)(2,1)S(1)} %get-tuple-element.55.refs_1_.refs_10_) | copy-start | bytes 1572868
  77.9 23.8 %collective-permute-start.5 = (bf16[128,2048]{1,0:T(8,128)(2,1)}, bf16[128,2048]{1,0:T(8,128)(2,1)S(1)}, u32[]{:S(2)}, u32[]{:S(2)}) collective-permute-start(bf16[128,2048]{1,0:T(8,128)(2,1)} %get-tuple-element.43), channel_id=1, source_target_pairs={{0,16},{16,32},{32,48},{48,0},{1,17},{17,33},{33,49},{49,1},{2,18}... | collective-permute-start | bytes 1572872 | tf_op jit(solution)/shard_map/ppermute | solution.py:497
  79.7 24.8 %collective-permute-start.6 = (bf16[128,2048]{1,0:T(8,128)(2,1)}, bf16[128,2048]{1,0:T(8,128)(2,1)S(1)}, u32[]{:S(2)}, u32[]{:S(2)}) collective-permute-start(bf16[128,2048]{1,0:T(8,128)(2,1)} %get-tuple-element.44), channel_id=1, source_target_pairs={{0,32},{16,48},{32,0},{48,16},{1,33},{17,49},{33,1},{49,17},{2,34}... | collective-permute-start | bytes 1572872 | tf_op jit(solution)/shard_map/ppermute | solution.py:497
  83.0 22.4 %collective-permute-start.7 = (bf16[128,2048]{1,0:T(8,128)(2,1)}, bf16[128,2048]{1,0:T(8,128)(2,1)S(1)}, u32[]{:S(2)}, u32[]{:S(2)}) collective-permute-start(bf16[128,2048]{1,0:T(8,128)(2,1)} %get-tuple-element.45), channel_id=1, source_target_pairs={{0,48},{16,0},{32,16},{48,32},{1,49},{17,1},{33,17},{49,33},{2,50}... | collective-permute-start | bytes 1572872 | tf_op jit(solution)/shard_map/ppermute | solution.py:497
  91.5 15.3 %collective-permute-start.3 = (bf16[256,1280]{1,0:T(8,128)(2,1)}, bf16[256,1280]{1,0:T(8,128)(2,1)}, u32[]{:S(2)}, u32[]{:S(2)}) collective-permute-start(bf16[256,1280]{1,0:T(8,128)(2,1)} %after.2), channel_id=1, source_target_pairs={{0,1},{1,0},{2,3},{3,2},{4,5},{5,4},{6,7},{7,6},{8,9},{9,8},{10,11... | collective-permute-start | bytes 1966088 | tf_op jit(solution)/shard_map/ppermute | solution.py:476
  93.0 8.0 %copy-start.16 = (f32[32]{0:T(128)S(1)}, f32[32]{0:T(128)}, u32[]{:S(2)}) copy-start(f32[32]{0:T(128)} %param.20) | copy-start | bytes 388
  99.0 14.6 %collective-permute-start.11 = (bf16[128,1920]{1,0:T(8,128)(2,1)}, bf16[128,1920]{1,0:T(8,128)(2,1)S(1)}, u32[]{:S(2)}, u32[]{:S(2)}) collective-permute-start(bf16[128,1920]{1,0:T(8,128)(2,1)} %get-tuple-element.52), channel_id=1, source_target_pairs={{0,16},{16,32},{32,48},{48,0},{1,17},{17,33},{33,49},{49,1},{2,18}... | collective-permute-start | bytes 1474568 | tf_op jit(solution)/shard_map/ppermute | solution.py:497
  101.6 23.9 %collective-permute-start.12 = (bf16[128,1920]{1,0:T(8,128)(2,1)}, bf16[128,1920]{1,0:T(8,128)(2,1)}, u32[]{:S(2)}, u32[]{:S(2)}) collective-permute-start(bf16[128,1920]{1,0:T(8,128)(2,1)} %copy-done.15), channel_id=1, source_target_pairs={{0,32},{16,48},{32,0},{48,16},{1,33},{17,49},{33,1},{49,17},{2,34}... | collective-permute-start | bytes 1474568 | tf_op jit(solution)/shard_map/ppermute | solution.py:497
  104.5 22.9 %collective-permute-start.13 = (bf16[128,1920]{1,0:T(8,128)(2,1)}, bf16[128,1920]{1,0:T(8,128)(2,1)}, u32[]{:S(2)}, u32[]{:S(2)}) collective-permute-start(bf16[128,1920]{1,0:T(8,128)(2,1)} %copy-done.14), channel_id=1, source_target_pairs={{0,48},{16,0},{32,16},{48,32},{1,49},{17,1},{33,17},{49,33},{2,50}... | collective-permute-start | bytes 1474568 | tf_op jit(solution)/shard_map/ppermute | solution.py:497
  105.4 11.0 %copy-start.2 = (bf16[128,2048]{1,0:T(8,128)(2,1)}, bf16[128,2048]{1,0:T(8,128)(2,1)S(1)}, u32[]{:S(2)}) copy-start(bf16[128,2048]{1,0:T(8,128)(2,1)S(1)} %collective-permute-done.7.refs_3_.refs_4_.refs_13_) | copy-start | bytes 1572868
  107.9 8.4 %copy-start.17 = (bf16[8,5120]{1,0:T(8,128)(2,1)S(1)}, bf16[8,5120]{1,0:T(8,128)(2,1)}, u32[]{:S(2)}) copy-start(bf16[8,5120]{1,0:T(8,128)(2,1)} %get-tuple-element.76) | copy-start | bytes 245764
  111.3 12.9 %copy-start.6 = (bf16[128,1280]{1,0:T(8,128)(2,1)}, bf16[128,1280]{1,0:T(8,128)(2,1)S(1)}, u32[]{:S(2)}) copy-start(bf16[128,1280]{1,0:T(8,128)(2,1)S(1)} %get-tuple-element.47.refs_8_.refs_1_) | copy-start | bytes 983044
  111.3 24.5 %collective-permute-start.10 = (bf16[128,1280]{1,0:T(8,128)(2,1)}, bf16[128,1280]{1,0:T(8,128)(2,1)}, u32[]{:S(2)}, u32[]{:S(2)}) collective-permute-start(bf16[128,1280]{1,0:T(8,128)(2,1)} %get-tuple-element.50), channel_id=1, source_target_pairs={{0,48},{16,0},{32,16},{48,32},{1,49},{17,1},{33,17},{49,33},{2,50}... | collective-permute-start | bytes 983048 | tf_op jit(solution)/shard_map/ppermute | solution.py:497
  112.8 23.0 %collective-permute-start.8 = (bf16[128,1280]{1,0:T(8,128)(2,1)}, bf16[128,1280]{1,0:T(8,128)(2,1)}, u32[]{:S(2)}, u32[]{:S(2)}) collective-permute-start(bf16[128,1280]{1,0:T(8,128)(2,1)} %get-tuple-element.48), channel_id=1, source_target_pairs={{0,16},{16,32},{32,48},{48,0},{1,17},{17,33},{33,49},{49,1},{2,18}... | collective-permute-start | bytes 983048 | tf_op jit(solution)/shard_map/ppermute | solution.py:497
  114.4 22.5 %collective-permute-start.9 = (bf16[128,1280]{1,0:T(8,128)(2,1)}, bf16[128,1280]{1,0:T(8,128)(2,1)}, u32[]{:S(2)}, u32[]{:S(2)}) collective-permute-start(bf16[128,1280]{1,0:T(8,128)(2,1)} %get-tuple-element.49), channel_id=1, source_target_pairs={{0,32},{16,48},{32,0},{48,16},{1,33},{17,49},{33,1},{49,17},{2,34}... | collective-permute-start | bytes 983048 | tf_op jit(solution)/shard_map/ppermute | solution.py:497
  116.4 11.0 %copy-start.11 = (bf16[128,1920]{1,0:T(8,128)(2,1)S(1)}, bf16[128,1920]{1,0:T(8,128)(2,1)}, u32[]{:S(2)}) copy-start(bf16[128,1920]{1,0:T(8,128)(2,1)} %copy-done.10) | copy-start | bytes 1474564
  116.4 11.0 %copy-start.13 = (bf16[128,1920]{1,0:T(8,128)(2,1)S(1)}, bf16[128,1920]{1,0:T(8,128)(2,1)}, u32[]{:S(2)}) copy-start(bf16[128,1920]{1,0:T(8,128)(2,1)} %copy-done.12) | copy-start | bytes 1474564
  127.4 9.5 %copy-start.5 = (bf16[128,2048]{1,0:T(8,128)(2,1)S(1)}, bf16[128,2048]{1,0:T(8,128)(2,1)}, u32[]{:S(2)}) copy-start(bf16[128,2048]{1,0:T(8,128)(2,1)} %copy-done.4) | copy-start | bytes 1572868
  127.4 9.5 %copy-start.7 = (bf16[128,1280]{1,0:T(8,128)(2,1)S(1)}, bf16[128,1280]{1,0:T(8,128)(2,1)}, u32[]{:S(2)}) copy-start(bf16[128,1280]{1,0:T(8,128)(2,1)} %copy-done.6) | copy-start | bytes 983044
  136.9 17.4 %copy-start.1 = (f32[32,2,5120]{2,1,0:T(2,128)S(1)}, f32[32,2,5120]{2,1,0:T(2,128)}, u32[]{:S(2)}) copy-start(f32[32,2,5120]{2,1,0:T(2,128)} %param.19) | copy-start | bytes 3932164
  144.3 5.3 %collective-permute-start.14 = (bf16[128,64]{1,0:T(8,128)(2,1)S(1)}, bf16[128,64]{1,0:T(8,128)(2,1)S(1)}, u32[]{:S(2)}, u32[]{:S(2)}) collective-permute-start(bf16[128,64]{1,0:T(8,128)(2,1)S(1)} %get-tuple-element.61), channel_id=1, source_target_pairs={{0,48},{16,0},{32,16},{48,32},{1,49},{17,1},{33,17},{49,33},{2,50}... | collective-permute-start | bytes 49160 | tf_op jit(solution)/shard_map/ppermute | solution.py:525
  148.3 4.3 %collective-permute-start.15 = (bf16[128,64]{1,0:T(8,128)(2,1)S(1)}, bf16[128,64]{1,0:T(8,128)(2,1)S(1)}, u32[]{:S(2)}, u32[]{:S(2)}) collective-permute-start(bf16[128,64]{1,0:T(8,128)(2,1)S(1)} %get-tuple-element.62), channel_id=1, source_target_pairs={{0,32},{16,48},{32,0},{48,16},{1,33},{17,49},{33,1},{49,17},{2,34}... | collective-permute-start | bytes 49160 | tf_op jit(solution)/shard_map/ppermute | solution.py:525
  149.4 4.0 %collective-permute-start.16 = (bf16[128,64]{1,0:T(8,128)(2,1)S(1)}, bf16[128,64]{1,0:T(8,128)(2,1)S(1)}, u32[]{:S(2)}, u32[]{:S(2)}) collective-permute-start(bf16[128,64]{1,0:T(8,128)(2,1)S(1)} %get-tuple-element.63), channel_id=1, source_target_pairs={{0,16},{16,32},{32,48},{48,0},{1,17},{17,33},{33,49},{49,1},{2,18}... | collective-permute-start | bytes 49160 | tf_op jit(solution)/shard_map/ppermute | solution.py:525
  (6 other events, 6.0 us)
Sparse Core Ops, SparseCore 0:
  13.3 30.8 all-gather.2
  48.3 62.7 all-gather.4
